TPU v7x, 32 devices: a whole 2x2x4 slice. The times are simulated.
32 devices in a mesh: mem: 8 (over z, x), head: 4 (over y, core).
Axes of the slice: x: 2, y: 2, z: 4, core: 2. Of those that a mesh axis runs over, the one named last changes fastest.
Arguments:
- query: bfloat16 [1024, 5120], P('mem', 'head'), may hold values from -96 to 96
- local_keys: bfloat16 [1024, 5120], P('mem', 'head'), may hold values from -6 to 6
- local_values: bfloat16 [1024, 5120], P('mem', 'head'), may hold values from -6 to 6
- mem_keys: bfloat16 [16384, 5120], P('mem', 'head'), may hold values from -4.5 to 4.5
- mem_values: bfloat16 [16384, 5120], P('mem', 'head'), may hold values from -6 to 6
- block_ids: int32 [8, 32], P('mem'), may hold values from 0 to 127, as said below
- out_proj: bfloat16 [5120, 5120], P('head'), may hold values from -1 to 1
- grad_out: bfloat16 [1024, 5120], P('mem', 'head'), may hold values from -6 to 6
Outputs:
- output: bfloat16 [1024, 5120], P('mem', 'head')
- grad_query: bfloat16 [1024, 5120], P('mem', 'head')
- grad_mem_keys: bfloat16 [16384, 5120], P('mem', 'head')
- grad_mem_values: bfloat16 [16384, 5120], P('mem', 'head')
Inputs may be any that keep to these rules, and one draw needn't show every extreme that they name: `block_ids`: each row names 32 different memory blocks. At most 6 of a row's blocks share one value of id // 16, and in every row exactly 6 share one value.
All inputs are finite; a program needn't handle non-finite values.
Results may differ from a plain program's by a relative error of at most 0.02.
Values may be sent and summed in bfloat16 or wider, within the bound.
A program may use at most 192 MiB of HBM per device.

v0:
```python
import jax
import jax.numpy as jnp
from jax import lax
from jax.sharding import PartitionSpec as P

HS = 128
BLOCK = 128
R = 32


lowest = -1e30


def owned_slots(id_row, holder, capacity, stored):
    is_owned = id_row // stored == holder
    order_rank = jnp.cumsum(is_owned.astype(jnp.int32)) - 1
    chosen = jnp.logical_and(
        is_owned[None, :], order_rank[None, :] == jnp.arange(capacity, dtype=jnp.int32)[:, None]
    )
    slots = jnp.sum(jnp.where(chosen, id_row[None, :] % stored, 0), axis=1).astype(jnp.int32)
    filled = jnp.any(chosen, axis=1)
    return (slots, filled)


def per_device(
    query, local_keys, local_values, mem_keys, mem_values, block_ids, out_proj, grad_out
):
    groups = lax.axis_size("mem")
    holder = lax.axis_index("mem")
    feature_width = query.shape[1]
    local_heads = feature_width // HS
    blocks = query.shape[0] // BLOCK
    stored = mem_keys.shape[0] // BLOCK
    capacity = R // groups + 2
    all_blocks = blocks * groups
    score_scale = HS ** (-0.5)
    causal = jnp.tril(jnp.ones((BLOCK, BLOCK), dtype=jnp.bool_))

    def heads_first(rows, count):
        return rows.reshape(count, BLOCK, local_heads, HS).transpose(0, 2, 1, 3)

    def rows_first(heads, count):
        return heads.transpose(0, 2, 1, 3).reshape(count * BLOCK, feature_width)

    query_heads = heads_first(query, blocks)
    near_keys = heads_first(local_keys, blocks)
    near_values = heads_first(local_values, blocks)
    key_store = mem_keys.reshape(stored, BLOCK, local_heads, HS).transpose(2, 0, 1, 3)
    value_store = mem_values.reshape(stored, BLOCK, local_heads, HS).transpose(2, 0, 1, 3)
    local_score = (
        jnp.einsum("bhqd,bhkd->bhqk", query_heads, near_keys, preferred_element_type=jnp.float32)
        * score_scale
    )
    local_score = jnp.where(causal, local_score, lowest)
    local_peak = jnp.max(local_score, axis=3)
    local_weight = jnp.where(causal, jnp.exp(local_score - local_peak[..., None]), 0.0)
    local_norm = jnp.sum(local_weight, axis=3)
    local_out = jnp.einsum(
        "bhqk,bhkd->bhqd",
        local_weight.astype(jnp.bfloat16),
        near_values,
        preferred_element_type=jnp.float32,
    )

    def select(id_row):
        slots, filled = owned_slots(id_row, holder, capacity, stored)
        chosen_keys = key_store[:, slots].reshape(local_heads, capacity * BLOCK, HS)
        chosen_values = value_store[:, slots].reshape(local_heads, capacity * BLOCK, HS)
        counted = jnp.repeat(filled, BLOCK)
        return (chosen_keys, chosen_values, counted, slots)

    def owner_forward(entry):
        query_rows, id_row = entry
        chosen_keys, chosen_values, counted, slots = select(id_row)
        scores = (
            jnp.einsum("hqd,hkd->hqk", query_rows, chosen_keys, preferred_element_type=jnp.float32)
            * score_scale
        )
        scores = jnp.where(counted, scores, lowest)
        peaks = jnp.max(scores, axis=2)
        weight = jnp.where(counted, jnp.exp(scores - peaks[..., None]), 0.0)
        partial_value = jnp.einsum(
            "hqk,hkd->hqd",
            weight.astype(jnp.bfloat16),
            chosen_values,
            preferred_element_type=jnp.float32,
        )
        return (partial_value, peaks, jnp.sum(weight, axis=2))

    zero_out = jnp.zeros((all_blocks, local_heads, BLOCK, HS), jnp.float32)
    zero_stat = jnp.zeros((all_blocks, local_heads, BLOCK), jnp.float32)
    zero_ids = jnp.zeros((all_blocks, R), jnp.int32)
    start_state = (zero_out, zero_stat, zero_stat, zero_ids)
    offset = jnp.int32(0)
    query_piece = lax.all_gather(query_heads, "mem", axis=0, tiled=True)
    id_piece = lax.all_gather(block_ids, "mem", axis=0, tiled=True)
    partial_value, peaks, norms = lax.map(owner_forward, (query_piece, id_piece))
    fresh_items = (partial_value, peaks, norms, id_piece, query_piece)
    folded = tuple(
        (
            lax.dynamic_update_slice_in_dim(earlier, fresh, offset, 0)
            for earlier, fresh in zip(start_state, fresh_items)
        )
    )
    part_out, part_peak, part_norm, all_ids = (folded[0], folded[1], folded[2], folded[3])
    got_out, got_peak, got_norm = (
        lax.all_to_all(part_out, "mem", split_axis=0, concat_axis=0, tiled=True),
        lax.all_to_all(part_peak, "mem", split_axis=0, concat_axis=0, tiled=True),
        lax.all_to_all(part_norm, "mem", split_axis=0, concat_axis=0, tiled=True),
    )
    got_out = got_out.reshape(groups, blocks, local_heads, BLOCK, HS)
    got_peak = got_peak.reshape(groups, blocks, local_heads, BLOCK)
    got_norm = got_norm.reshape(groups, blocks, local_heads, BLOCK)
    peaks = jnp.maximum(jnp.max(got_peak, axis=0), local_peak)
    factor = jnp.exp(got_peak - peaks)
    own_factor = jnp.exp(local_peak - peaks)
    mixed = jnp.sum(got_out * factor[..., None], axis=0) + local_out * own_factor[..., None]
    norms = jnp.sum(got_norm * factor, axis=0) + local_norm * own_factor
    attention = (mixed / norms[..., None]).astype(jnp.bfloat16)
    log_norm = peaks + jnp.log(norms)
    projected = jnp.dot(rows_first(attention, blocks), out_proj, preferred_element_type=jnp.float32)
    output = lax.psum_scatter(
        projected.astype(jnp.bfloat16), "head", scatter_dimension=1, tiled=True
    )
    d_attention = lax.dot_general(
        lax.all_gather(grad_out, "head", axis=1, tiled=True),
        out_proj,
        (((1,), (1,)), ((), ())),
        preferred_element_type=jnp.float32,
    ).astype(jnp.bfloat16)
    grad_heads = heads_first(d_attention, blocks)
    deltas = jnp.sum(grad_heads.astype(jnp.float32) * attention.astype(jnp.float32), axis=3)
    local_prob = jnp.where(causal, jnp.exp(local_score - log_norm[..., None]), 0.0)
    local_prob_grad = jnp.einsum(
        "bhqd,bhkd->bhqk", grad_heads, near_values, preferred_element_type=jnp.float32
    )
    local_score_grad = (local_prob * (local_prob_grad - deltas[..., None])).astype(jnp.bfloat16)
    local_query_grad = (
        jnp.einsum(
            "bhqk,bhkd->bhqd", local_score_grad, near_keys, preferred_element_type=jnp.float32
        )
        * score_scale
    )
    row_norms, row_deltas = (
        lax.all_gather(log_norm, "mem", axis=0, tiled=True),
        lax.all_gather(deltas, "mem", axis=0, tiled=True),
    )

    def owner_backward(running, entry):
        key_grad, value_grad = running
        query_part, grad_part, norm_rows, delta_rows, id_row = entry
        chosen_keys, chosen_values, counted, slots = select(id_row)
        scores = (
            jnp.einsum("hqd,hkd->hqk", query_part, chosen_keys, preferred_element_type=jnp.float32)
            * score_scale
        )
        prob = jnp.where(counted, jnp.exp(scores - norm_rows[..., None]), 0.0)
        prob_grad = jnp.einsum(
            "hqd,hkd->hqk", grad_part, chosen_values, preferred_element_type=jnp.float32
        )
        score_grad = (prob * (prob_grad - delta_rows[..., None])).astype(jnp.bfloat16)
        query_grad = (
            jnp.einsum("hqk,hkd->hqd", score_grad, chosen_keys, preferred_element_type=jnp.float32)
            * score_scale
        )
        key_part = (
            jnp.einsum("hqk,hqd->hkd", score_grad, query_part, preferred_element_type=jnp.float32)
            * score_scale
        )
        value_part = jnp.einsum(
            "hqk,hqd->hkd", prob.astype(jnp.bfloat16), grad_part, preferred_element_type=jnp.float32
        )
        key_grad = key_grad.at[:, slots].add(key_part.reshape(local_heads, capacity, BLOCK, HS))
        value_grad = value_grad.at[:, slots].add(
            value_part.reshape(local_heads, capacity, BLOCK, HS)
        )
        return ((key_grad, value_grad), query_grad)

    zero_store = jnp.zeros((local_heads, stored, BLOCK, HS), jnp.float32)
    key_grad = zero_store
    value_grad = zero_store
    id_piece = all_ids
    (key_grad, value_grad), piece_grad = lax.scan(
        owner_backward,
        (key_grad, value_grad),
        (
            lax.all_gather(query_heads, "mem", axis=0, tiled=True),
            lax.all_gather(grad_heads, "mem", axis=0, tiled=True),
            row_norms,
            row_deltas,
            id_piece,
        ),
    )
    query_grads = piece_grad
    query_grads, key_grad, value_grad = (query_grads, key_grad, value_grad)
    mine_grads = lax.psum_scatter(
        query_grads.astype(jnp.bfloat16), "mem", scatter_dimension=0, tiled=True
    ).astype(jnp.float32)
    grad_query = rows_first(mine_grads + local_query_grad, blocks).astype(jnp.bfloat16)
    grad_mem_keys = (
        key_grad.transpose(1, 2, 0, 3).reshape(stored * BLOCK, feature_width).astype(jnp.bfloat16)
    )
    grad_mem_values = (
        value_grad.transpose(1, 2, 0, 3).reshape(stored * BLOCK, feature_width).astype(jnp.bfloat16)
    )
    return (output, grad_query, grad_mem_keys, grad_mem_values)


def solution(mesh):
    placed = (
        P("mem", "head"),
        P("mem", "head"),
        P("mem", "head"),
        P("mem", "head"),
        P("mem", "head"),
        P("mem", None),
        P("head", None),
        P("mem", "head"),
    )
    return jax.shard_map(
        per_device,
        mesh=mesh,
        in_specs=placed,
        out_specs=(P("mem", "head"), P("mem", "head"), P("mem", "head"), P("mem", "head")),
        check_vma=False,
    )
```

profile of v0, /device:TPU:0, one launch (start us, length us, event | category | flops | bytes accessed | tf_op | source)
XLA Modules:
  0.0 880.1 jit_solution(3943965763030001873)
XLA Ops:
  10.2 7.9 copy.142
  18.1 6.6 copy.185
  24.7 8.6 copy.144
  33.3 8.0 copy.143
  41.3 6.9 copy.186
  48.2 8.7 copy.145
  56.9 21.9 %all-gather.1 = s32[8,1,32]{2,1,0:T(1,128)S(1)} all-gather(s32[1,1,32]{2,1,0:T(1,128)S(1)} %bitcast.287), channel_id=1, replica_groups=mesh['mem'=8,'head'=4] {'mem'}, dimensions={0}, use_global_device_ids=true | all-gather | bytes 1152 | tf_op jit(solution)/shard_map/all_gather | solution.py:96
  78.8 122.6 %while.34 = (s32[]{:T(128)}, f32[8,10,128,128]{3,2,1,0:T(8,128)}, f32[8,10,128]{2,1,0:T(8,128)S(1)}, f32[8,10,128]{2,1,0:T(8,128)S(1)}, s32[8,32]{1,0:T(8,128)S(...) while((s32[]{:T(128)}, f32[8,10,128,128]{3,2,1,0:T(8,128)}, ...), condition=%wide.region_6.7_spmd, body=%wide.region_0.6_spmd.sunk | while | flops 516097568 | bytes 40367528 | solution.py:97
  201.4 9.3 %all_to_all.15 = f32[8,10,128]{2,1,0:T(8,128)S(1)} all-to-all(f32[8,10,128]{2,1,0:T(8,128)S(1)} %get-tuple-element.344), channel_id=1, replica_groups=mesh['mem'=8,'head'=4] {'mem'}, dimensions={0} | all-to-all | bytes 81920 | tf_op jit(solution)/shard_map/all_to_all | solution.py:109
  210.7 9.3 %all_to_all.16 = f32[8,10,128]{2,1,0:T(8,128)S(1)} all-to-all(f32[8,10,128]{2,1,0:T(8,128)S(1)} %get-tuple-element.343), channel_id=1, replica_groups=mesh['mem'=8,'head'=4] {'mem'}, dimensions={0} | all-to-all | bytes 81920 | tf_op jit(solution)/shard_map/all_to_all | solution.py:108
  219.9 4.6 all-to-all-start
  225.5 20.5 %all-gather.9.cloned.1.call-done = bf16[128,5120]{1,0:T(8,128)(2,1)} async-done(((bf16[128,1280]{1,0:T(8,128)(2,1)}), bf16[128,5120]{1,0:T(8,128)(2,1)}) %all-gather.9.cloned.1.call-update) | async-done | bytes 1310736 | tf_op jit(solution)/shard_map/all_gather | solution.py:126
  246.0 9.5 %convolution_convert_fusion.1 = bf16[128,1280]{1,0:T(8,128)(2,1)S(1)} fusion(bf16[128,5120]{1,0:T(8,128)(2,1)} %all-gather.9.cloned.1.call-done, bf16[1280,5120]{1,0:T(8,128)(2,1)} %param.18), kind=kOutput, calls=%fused_computation.103 | convolution fusion | flops 1677885440 | bytes 14745600 | tf_op jit(solution)/shard_map/dot_general | solution.py:125
  257.8 128.1 %all_gather.21 = f32[8,10,128]{2,1,0:T(8,128)S(1)} all-gather(f32[1,10,128]{2,1,0:T(8,128)S(1)} %fusion.80), channel_id=1, replica_groups=mesh['mem'=8,'head'=4] {'mem'}, dimensions={0}, use_global_device_ids=true | all-gather | bytes 46080 | tf_op jit(solution)/shard_map/all_gather | solution.py:145
  390.6 30.5 %all-gather.2 = f32[8,10,128]{2,1,0:T(8,128)S(1)} all-gather(f32[1,10,128]{2,1,0:T(8,128)S(1)} %bitcast.286), channel_id=2, replica_groups=mesh['mem'=8,'head'=4] {'mem'}, dimensions={0}, use_global_device_ids=true | all-gather | bytes 46080 | tf_op jit(solution)/shard_map/all_gather | solution.py:146
  421.1 5.2 broadcast_in_dim.181.clone
  426.2 5.3 broadcast_in_dim.181
  431.6 343.4 %while.35 = (s32[]{:T(128)}, f32[10,16,128,128]{3,2,1,0:T(8,128)}, f32[10,16,128,128]{3,2,1,0:T(8,128)}, bf16[8,10,128,128]{2,3,1,0:T(8,128)(2,1)}, s32[8,32]{1,...) while((s32[]{:T(128)}, f32[10,16,128,128]{3,2,1,0:T(8,128)}, ...), condition=%wide.region_20.21_spmd, body=%wide.region_14.20_spmd.sunk | while | flops 1271402496 | bytes 97365752 | solution.py:183
  432.2 3.4 gather_fusion.3
  455.1 9.5 %scatter_fusion = f32[10,16,128,128]{3,2,1,0:T(8,128)} fusion(f32[10,16,128,128]{3,2,1,0:T(8,128)} %get-tuple-element.729, s32[6]{0:T(128)S(1)} %fusion.151, f32[6,10,128,128]{3,2,1,0:T(8,128)} %bitcast.257), kind=kCustom, calls=%fused_computation.4.clone.1 | custom fusion | flops 983040 | bytes 11796504 | tf_op jit(solution)/shard_map/while/body/eval_jaxpr/scatter-add | solution.py:173
  464.6 9.5 %scatter_fusion.1 = f32[10,16,128,128]{3,2,1,0:T(8,128)} fusion(f32[10,16,128,128]{3,2,1,0:T(8,128)} %get-tuple-element.730, s32[6]{0:T(128)S(1)} %fusion.151, f32[6,10,128,128]{3,2,1,0:T(8,128)} %bitcast.256), kind=kCustom, calls=%fused_computation.5.clone.1 | custom fusion | flops 983040 | bytes 11796504 | tf_op jit(solution)/shard_map/while/body/eval_jaxpr/scatter-add | solution.py:174
  474.7 3.4 gather_fusion.3
  497.6 9.7 %scatter_fusion = f32[10,16,128,128]{3,2,1,0:T(8,128)} fusion(f32[10,16,128,128]{3,2,1,0:T(8,128)} %get-tuple-element.729, s32[6]{0:T(128)S(1)} %fusion.151, f32[6,10,128,128]{3,2,1,0:T(8,128)} %bitcast.257), kind=kCustom, calls=%fused_computation.4.clone.1 | custom fusion | flops 983040 | bytes 11796504 | tf_op jit(solution)/shard_map/while/body/eval_jaxpr/scatter-add | solution.py:173
  507.3 9.7 %scatter_fusion.1 = f32[10,16,128,128]{3,2,1,0:T(8,128)} fusion(f32[10,16,128,128]{3,2,1,0:T(8,128)} %get-tuple-element.730, s32[6]{0:T(128)S(1)} %fusion.151, f32[6,10,128,128]{3,2,1,0:T(8,128)} %bitcast.256), kind=kCustom, calls=%fused_computation.5.clone.1 | custom fusion | flops 983040 | bytes 11796504 | tf_op jit(solution)/shard_map/while/body/eval_jaxpr/scatter-add | solution.py:174
  517.6 3.4 gather_fusion.3
  540.6 9.7 %scatter_fusion = f32[10,16,128,128]{3,2,1,0:T(8,128)} fusion(f32[10,16,128,128]{3,2,1,0:T(8,128)} %get-tuple-element.729, s32[6]{0:T(128)S(1)} %fusion.151, f32[6,10,128,128]{3,2,1,0:T(8,128)} %bitcast.257), kind=kCustom, calls=%fused_computation.4.clone.1 | custom fusion | flops 983040 | bytes 11796504 | tf_op jit(solution)/shard_map/while/body/eval_jaxpr/scatter-add | solution.py:173
  550.3 9.7 %scatter_fusion.1 = f32[10,16,128,128]{3,2,1,0:T(8,128)} fusion(f32[10,16,128,128]{3,2,1,0:T(8,128)} %get-tuple-element.730, s32[6]{0:T(128)S(1)} %fusion.151, f32[6,10,128,128]{3,2,1,0:T(8,128)} %bitcast.256), kind=kCustom, calls=%fused_computation.5.clone.1 | custom fusion | flops 983040 | bytes 11796504 | tf_op jit(solution)/shard_map/while/body/eval_jaxpr/scatter-add | solution.py:174
  560.6 3.4 gather_fusion.3
  583.4 9.9 %scatter_fusion = f32[10,16,128,128]{3,2,1,0:T(8,128)} fusion(f32[10,16,128,128]{3,2,1,0:T(8,128)} %get-tuple-element.729, s32[6]{0:T(128)S(1)} %fusion.151, f32[6,10,128,128]{3,2,1,0:T(8,128)} %bitcast.257), kind=kCustom, calls=%fused_computation.4.clone.1 | custom fusion | flops 983040 | bytes 11796504 | tf_op jit(solution)/shard_map/while/body/eval_jaxpr/scatter-add | solution.py:173
  593.3 10.0 %scatter_fusion.1 = f32[10,16,128,128]{3,2,1,0:T(8,128)} fusion(f32[10,16,128,128]{3,2,1,0:T(8,128)} %get-tuple-element.730, s32[6]{0:T(128)S(1)} %fusion.151, f32[6,10,128,128]{3,2,1,0:T(8,128)} %bitcast.256), kind=kCustom, calls=%fused_computation.5.clone.1 | custom fusion | flops 983040 | bytes 11796504 | tf_op jit(solution)/shard_map/while/body/eval_jaxpr/scatter-add | solution.py:174
  604.0 3.4 gather_fusion.3
  626.8 9.7 %scatter_fusion = f32[10,16,128,128]{3,2,1,0:T(8,128)} fusion(f32[10,16,128,128]{3,2,1,0:T(8,128)} %get-tuple-element.729, s32[6]{0:T(128)S(1)} %fusion.151, f32[6,10,128,128]{3,2,1,0:T(8,128)} %bitcast.257), kind=kCustom, calls=%fused_computation.4.clone.1 | custom fusion | flops 983040 | bytes 11796504 | tf_op jit(solution)/shard_map/while/body/eval_jaxpr/scatter-add | solution.py:173
  636.5 9.7 %scatter_fusion.1 = f32[10,16,128,128]{3,2,1,0:T(8,128)} fusion(f32[10,16,128,128]{3,2,1,0:T(8,128)} %get-tuple-element.730, s32[6]{0:T(128)S(1)} %fusion.151, f32[6,10,128,128]{3,2,1,0:T(8,128)} %bitcast.256), kind=kCustom, calls=%fused_computation.5.clone.1 | custom fusion | flops 983040 | bytes 11796504 | tf_op jit(solution)/shard_map/while/body/eval_jaxpr/scatter-add | solution.py:174
  669.8 9.7 %scatter_fusion = f32[10,16,128,128]{3,2,1,0:T(8,128)} fusion(f32[10,16,128,128]{3,2,1,0:T(8,128)} %get-tuple-element.729, s32[6]{0:T(128)S(1)} %fusion.151, f32[6,10,128,128]{3,2,1,0:T(8,128)} %bitcast.257), kind=kCustom, calls=%fused_computation.4.clone.1 | custom fusion | flops 983040 | bytes 11796504 | tf_op jit(solution)/shard_map/while/body/eval_jaxpr/scatter-add | solution.py:173
  679.5 9.7 %scatter_fusion.1 = f32[10,16,128,128]{3,2,1,0:T(8,128)} fusion(f32[10,16,128,128]{3,2,1,0:T(8,128)} %get-tuple-element.730, s32[6]{0:T(128)S(1)} %fusion.151, f32[6,10,128,128]{3,2,1,0:T(8,128)} %bitcast.256), kind=kCustom, calls=%fused_computation.5.clone.1 | custom fusion | flops 983040 | bytes 11796504 | tf_op jit(solution)/shard_map/while/body/eval_jaxpr/scatter-add | solution.py:174
  689.8 3.4 gather_fusion.3
  712.7 9.7 %scatter_fusion = f32[10,16,128,128]{3,2,1,0:T(8,128)} fusion(f32[10,16,128,128]{3,2,1,0:T(8,128)} %get-tuple-element.729, s32[6]{0:T(128)S(1)} %fusion.151, f32[6,10,128,128]{3,2,1,0:T(8,128)} %bitcast.257), kind=kCustom, calls=%fused_computation.4.clone.1 | custom fusion | flops 983040 | bytes 11796504 | tf_op jit(solution)/shard_map/while/body/eval_jaxpr/scatter-add | solution.py:173
  722.4 9.7 %scatter_fusion.1 = f32[10,16,128,128]{3,2,1,0:T(8,128)} fusion(f32[10,16,128,128]{3,2,1,0:T(8,128)} %get-tuple-element.730, s32[6]{0:T(128)S(1)} %fusion.151, f32[6,10,128,128]{3,2,1,0:T(8,128)} %bitcast.256), kind=kCustom, calls=%fused_computation.5.clone.1 | custom fusion | flops 983040 | bytes 11796504 | tf_op jit(solution)/shard_map/while/body/eval_jaxpr/scatter-add | solution.py:174
  755.6 9.7 %scatter_fusion = f32[10,16,128,128]{3,2,1,0:T(8,128)} fusion(f32[10,16,128,128]{3,2,1,0:T(8,128)} %get-tuple-element.729, s32[6]{0:T(128)S(1)} %fusion.151, f32[6,10,128,128]{3,2,1,0:T(8,128)} %bitcast.257), kind=kCustom, calls=%fused_computation.4.clone.1 | custom fusion | flops 983040 | bytes 11796504 | tf_op jit(solution)/shard_map/while/body/eval_jaxpr/scatter-add | solution.py:173
  765.3 9.7 %scatter_fusion.1 = f32[10,16,128,128]{3,2,1,0:T(8,128)} fusion(f32[10,16,128,128]{3,2,1,0:T(8,128)} %get-tuple-element.730, s32[6]{0:T(128)S(1)} %fusion.151, f32[6,10,128,128]{3,2,1,0:T(8,128)} %bitcast.256), kind=kCustom, calls=%fused_computation.5.clone.1 | custom fusion | flops 983040 | bytes 11796504 | tf_op jit(solution)/shard_map/while/body/eval_jaxpr/scatter-add | solution.py:174
  775.1 7.7 convolution_convert_fusion
  782.8 21.0 %convert_bitcast_fusion = (bf16[16,128,10,128]{3,1,0,2:T(8,128)(2,1)}, bf16[16,128,10,128]{3,1,0,2:T(8,128)(2,1)}) fusion(f32[10,16,128,128]{3,2,1,0:T(8,128)} %get-tuple-element.347, f32[10,16,128,128]{3,2,1,0:T(8,128)} %get-tuple-element.346), kind=kLoop, calls=%fused_computation.100 | loop fusion | flops 5242880 | bytes 31457280 | tf_op jit(solution)/shard_map/convert_element_type | solution.py:204
  803.8 7.2 copy.176
  811.0 5.0 copy.195
  816.0 7.4 copy.175
  823.5 5.1 copy.196
  828.6 15.6 %reduce-scatter.5.cloned.1.call-done = bf16[1,10,128,128]{2,3,1,0:T(8,128)(2,1)} async-done(((bf16[8,10,128,128]{2,3,1,0:T(8,128)(2,1)}), bf16[1,10,128,128]{2,3,1,0:T(8,128)(2,1)}) %reduce-scatter.5.cloned.1.call-update) | async-done | bytes 327696 | tf_op jit(solution)/shard_map/reduce_scatter | solution.py:196
  846.7 26.1 %reduce-scatter.3.cloned.1.call-done = bf16[128,1280]{1,0:T(8,128)(2,1)} async-done(((bf16[128,5120]{1,0:T(8,128)(2,1)}), bf16[128,1280]{1,0:T(8,128)(2,1)}) %reduce-scatter.3.cloned.1.call-update) | async-done | bytes 327696 | tf_op jit(solution)/shard_map/reduce_scatter | solution.py:122
  (446 shorter events, 300.9 us)
Async XLA Ops:
  8.0 70.8 %all-gather.7.cloned.1.call-start = ((), (), s32[]{:S(2)}) async-start(), calls=%async_computation.5 | async-start | bytes 2949120 | tf_op jit(solution)/shard_map/all_gather | solution.py:95
  48.2 8.7 copy-start.17
  87.7 1.5 copy-start
  103.0 1.5 copy-start
  118.3 1.5 copy-start
  133.6 1.5 copy-start
  149.0 1.5 copy-start
  164.3 1.5 copy-start
  179.6 1.5 copy-start
  194.9 1.5 copy-start
  219.9 166.7 %all-to-all-start = ((f32[8,10,128,128]{3,2,1,0:T(8,128)}), f32[8,10,128,128]{3,2,1,0:T(8,128)}, u32[]{:S(2)}, u32[]{:S(2)}) async-start(f32[8,10,128,128]{3,2,1,0:T(8,128)} %get-tuple-element.342), calls=%async_computation | async-start | bytes 10485760 | tf_op jit(solution)/shard_map/all_to_all | solution.py:107
  224.6 21.4 %all-gather.9.cloned.1.call-start = ((), (), s32[]{:S(2)}) async-start(), calls=%async_computation.7 | async-start | bytes 1638400 | tf_op jit(solution)/shard_map/all_gather | solution.py:126
  225.2 31.6 %copy-start.8 = (bf16[128,1280]{1,0:T(8,128)(2,1)S(1)}, bf16[128,1280]{1,0:T(8,128)(2,1)}, u32[]{:S(2)}) copy-start(bf16[128,1280]{1,0:T(8,128)(2,1)} %param.13) | copy-start | bytes 983044
  225.2 31.8 %copy-start.9 = (bf16[128,1280]{1,0:T(8,128)(2,1)S(1)}, bf16[128,1280]{1,0:T(8,128)(2,1)}, u32[]{:S(2)}) copy-start(bf16[128,1280]{1,0:T(8,128)(2,1)} %param.14) | copy-start | bytes 983044
  225.2 195.9 %all-gather.11.cloned.1.call-start = ((), (), s32[]{:S(2)}) async-start(), calls=%async_computation.8 | async-start | bytes 2949120 | tf_op jit(solution)/shard_map/all_gather | solution.py:188
  255.8 134.4 %copy-start.4 = (bf16[128,1280]{0,1:T(8,128)(2,1)}, bf16[128,1280]{0,1:T(8,128)(2,1)S(1)}, u32[]{:S(2)}) copy-start(bf16[128,1280]{0,1:T(8,128)(2,1)S(1)} %copy.152) | copy-start | bytes 983044
  256.7 587.5 %reduce-scatter.5.cloned.1.call-start = ((), (), s32[]{:S(2)}) async-start(), calls=%async_computation.9 | async-start | bytes 2949120 | tf_op jit(solution)/shard_map/reduce_scatter | solution.py:196
  257.0 132.9 %copy-start.6 = (bf16[128,1280]{0,1:T(8,128)(2,1)}, bf16[128,1280]{0,1:T(8,128)(2,1)S(1)}, u32[]{:S(2)}) copy-start(bf16[128,1280]{0,1:T(8,128)(2,1)S(1)} %copy.146) | copy-start | bytes 983044
  257.2 133.0 %copy-start.10 = (bf16[128,1280]{0,1:T(8,128)(2,1)}, bf16[128,1280]{0,1:T(8,128)(2,1)S(1)}, u32[]{:S(2)}) copy-start(bf16[128,1280]{0,1:T(8,128)(2,1)S(1)} %copy.149) | copy-start | bytes 983044
  257.3 132.9 %copy-start.12 = (pred[128,128]{0,1:T(8,128)(4,1)}, pred[128,128]{0,1:T(8,128)(4,1)S(1)}, u32[]{:S(2)}) copy-start(pred[128,128]{0,1:T(8,128)(4,1)S(1)} %iota_compare_fusion.2) | copy-start | bytes 49156
  257.6 132.6 %copy-start.2 = (f32[10,128,128]{1,2,0:T(8,128)}, f32[10,128,128]{1,2,0:T(8,128)S(1)}, u32[]{:S(2)}) copy-start(f32[10,128,128]{1,2,0:T(8,128)S(1)} %get-tuple-element.524) | copy-start | bytes 1966084
  390.6 35.7 %copy-start.15 = (f32[10,128]{1,0:T(8,128)}, f32[10,128]{1,0:T(8,128)S(1)}, u32[]{:S(2)}) copy-start(f32[10,128]{1,0:T(8,128)S(1)} %get-tuple-element.525) | copy-start | bytes 15364
  440.6 1.8 copy-start.1
  483.1 1.8 copy-start.1
  526.0 1.8 copy-start.1
  569.0 1.8 copy-start.1
  612.3 1.8 copy-start.1
  655.3 1.8 copy-start.1
  698.2 1.8 copy-start.1
  741.1 1.8 copy-start.1
  775.0 97.7 %reduce-scatter.3.cloned.1.call-start = ((), (), s32[]{:S(2)}) async-start(), calls=%async_computation.6 | async-start | bytes 1638400 | tf_op jit(solution)/shard_map/reduce_scatter | solution.py:122
  823.5 20.8 %copy-start.3 = (f32[10,128,128]{1,2,0:T(8,128)S(1)}, f32[10,128,128]{1,2,0:T(8,128)}, u32[]{:S(2)}) copy-start(f32[10,128,128]{1,2,0:T(8,128)} %copy-done.2) | copy-start | bytes 1966084
  823.5 20.8 %copy-start.5 = (bf16[128,1280]{0,1:T(8,128)(2,1)S(1)}, bf16[128,1280]{0,1:T(8,128)(2,1)}, u32[]{:S(2)}) copy-start(bf16[128,1280]{0,1:T(8,128)(2,1)} %copy-done.4) | copy-start | bytes 983044
  823.5 20.8 %copy-start.7 = (bf16[128,1280]{0,1:T(8,128)(2,1)S(1)}, bf16[128,1280]{0,1:T(8,128)(2,1)}, u32[]{:S(2)}) copy-start(bf16[128,1280]{0,1:T(8,128)(2,1)} %copy-done.6) | copy-start | bytes 983044
  823.5 20.8 %copy-start.11 = (bf16[128,1280]{0,1:T(8,128)(2,1)S(1)}, bf16[128,1280]{0,1:T(8,128)(2,1)}, u32[]{:S(2)}) copy-start(bf16[128,1280]{0,1:T(8,128)(2,1)} %copy-done.10) | copy-start | bytes 983044
  823.5 20.8 %copy-start.13 = (pred[128,128]{0,1:T(8,128)(4,1)S(1)}, pred[128,128]{0,1:T(8,128)(4,1)}, u32[]{:S(2)}) copy-start(pred[128,128]{0,1:T(8,128)(4,1)} %copy-done.12) | copy-start | bytes 49156
  823.5 20.8 %copy-start.14 = (f32[10,128]{1,0:T(8,128)S(1)}, f32[10,128]{1,0:T(8,128)}, u32[]{:S(2)}) copy-start(f32[10,128]{1,0:T(8,128)} %get-tuple-element.512) | copy-start | bytes 15364
  823.5 20.8 %copy-start.16 = (f32[10,128]{1,0:T(8,128)S(1)}, f32[10,128]{1,0:T(8,128)}, u32[]{:S(2)}) copy-start(f32[10,128]{1,0:T(8,128)} %copy-done.15) | copy-start | bytes 15364
Sparse Core Ops, SparseCore 0:
  11.6 57.3 all-gather.6
  256.9 111.4 all-gather.10
  775.1 69.0 reduce-scatter.4
  847.2 25.4 reduce-scatter.2
Sparse Core Ops, SparseCore 1:
  226.6 19.3 all-gather.8
where the time goes:
time: 892 us; the launch traced here: 880 us
  local copies, waits for them, and re-layouts  280 us (31%)
  blocking collectives  199 us (22%)
  other arithmetic  197 us (22%)
  matrix products  119 us (13%)
  waiting for transfers between devices  62.8 us (7%)
  between operations  15.8 us (2%)
    all_gather x1, blocking collectives, per_device(): lax.all_gather(log_norm, 'mem', axis=0, tiled=True)  128 us
    scatter-add x8, other arithmetic, owner_backward(): value_grad.at[:, slots]  77.7 us
    scatter-add x8, other arithmetic, owner_backward(): key_grad.at[:, slots]  77.6 us
    gather x32, local copies, waits for them, and re-layouts, select(): value_store[:, slots].reshape(local_heads, capacity * BLOCK, HS)  67.5 us
    gather x32, local copies, waits for them, and re-layouts, select(): chosen_keys = key_store[:, slots].reshape(local_heads, capacity * BLOCK, HS)  66.7 us
    unnamed x44, local copies, waits for them, and re-layouts  56.7 us
    all_gather x1, blocking collectives, per_device(): lax.all_gather(deltas, 'mem', axis=0, tiled=True)  30.5 us
    reduce_scatter x1, waiting for transfers between devices, per_device(): lax.psum_scatter(projected.astype(jnp.bfloat16), 'head', scatter_dimensio...  26.1 us
  transfers between devices with their start and end apart: 6, of which 3 were waited for; matrix products, arithmetic and copies ran while one was open for 13% of the time, Pallas kernels for 0%

commit v1 on v0

v1 whole, which is shorter than its diff:
```python
import functools
import math

import jax
import jax.numpy as jnp
from jax import lax
from jax.experimental import pallas as pl
from jax.experimental.pallas import tpu as pltpu
from jax.sharding import PartitionSpec as P

HS = 128
BLOCK = 128
R = 32
STAT_ROWS = 16
LOWEST = -1e30
SCALE = HS ** (-0.5)
LOG2E = math.log2(math.e)
F32 = jnp.float32
BF16 = jnp.bfloat16
VMEM_LIMIT = 56 * 1024 * 1024


def dot_last(a, b):
    return lax.dot_general(a, b, (((1,), (1,)), ((), ())), preferred_element_type=F32)


def dot_plain(a, b):
    return lax.dot_general(a, b, (((1,), (0,)), ((), ())), preferred_element_type=F32)


def owned_slots(ids, holder, capacity, stored):
    is_owned = ids // stored == holder
    rank = jnp.cumsum(is_owned.astype(jnp.int32), axis=1) - 1
    chosen = jnp.logical_and(
        is_owned[:, None, :], rank[:, None, :] == jnp.arange(capacity, dtype=jnp.int32)[None, :, None]
    )
    slots = jnp.sum(jnp.where(chosen, (ids % stored)[:, None, :], 0), axis=2).astype(jnp.int32)
    count = jnp.sum(is_owned.astype(jnp.int32), axis=1, keepdims=True)
    return jnp.concatenate([slots, count], axis=1)


def by_count(count, capacity, body):
    small = capacity - 2
    if small < 3:
        body(capacity)
        return
    pl.when(count <= small)(lambda: body(small))
    pl.when(count > small)(lambda: body(capacity))


def forward_kernel(blocks, capacity, stored, slots_ref, q_ref, k_ref, v_ref, out_ref, stat_ref, vt_ref):
    head = pl.program_id(0)
    for m in range(stored):
        vt_ref[m] = v_ref[m * BLOCK : (m + 1) * BLOCK, :].T

    def one_block(b, carry):
        count = slots_ref[b, capacity]
        q = q_ref[pl.ds(pl.multiple_of(b * BLOCK, BLOCK), BLOCK), :]

        def body(n):
            scores = []
            peak = jnp.full((1, BLOCK), LOWEST, F32)
            for j in range(n):
                slot = slots_ref[b, j]
                keys = k_ref[pl.ds(pl.multiple_of(slot * BLOCK, BLOCK), BLOCK), :]
                s = dot_last(keys, q) * (SCALE * LOG2E)
                s = jnp.where(j < count, s, LOWEST)
                scores.append(s)
            top = functools.reduce(jnp.maximum, scores)
            peak = jnp.max(top, axis=0, keepdims=True)
            weights = [jnp.exp2(s - peak) for s in scores]
            norm = jnp.sum(functools.reduce(jnp.add, weights), axis=0, keepdims=True)
            total = None
            for j in range(n):
                term = dot_plain(vt_ref[slots_ref[b, j]], weights[j].astype(BF16))
                total = term if total is None else total + term
            out_ref[b, 0] = total.astype(BF16)
            stat_ref[b, 0, pl.ds(head, 1), :] = peak
            stat_ref[b, 1, pl.ds(head, 1), :] = norm

        by_count(count, capacity, body)
        return carry

    lax.fori_loop(0, blocks, one_block, 0)


def holder_forward(slots, q_all, keys, values, capacity):
    rows, width = q_all.shape
    heads, blocks, stored = width // HS, rows // BLOCK, keys.shape[0] // BLOCK
    column = lambda n: pl.BlockSpec((n, HS), lambda h, s: (0, h))
    return pl.pallas_call(
        functools.partial(forward_kernel, blocks, capacity, stored),
        grid_spec=pltpu.PrefetchScalarGridSpec(
            num_scalar_prefetch=1,
            grid=(heads,),
            in_specs=[column(rows), column(stored * BLOCK), column(stored * BLOCK)],
            out_specs=[
                pl.BlockSpec((blocks, 1, HS, BLOCK), lambda h, s: (0, h, 0, 0)),
                pl.BlockSpec((blocks, 2, STAT_ROWS, BLOCK), lambda h, s: (0, 0, 0, 0)),
            ],
            scratch_shapes=[pltpu.VMEM((stored, HS, BLOCK), BF16)],
        ),
        out_shape=[
            jax.ShapeDtypeStruct((blocks, heads, HS, BLOCK), BF16),
            jax.ShapeDtypeStruct((blocks, 2, STAT_ROWS, BLOCK), F32),
        ],
        compiler_params=pltpu.CompilerParams(vmem_limit_bytes=VMEM_LIMIT),
        cost_estimate=pl.CostEstimate(flops=4 * 10**9, bytes_accessed=16 * 10**6, transcendentals=0),
    )(slots, q_all, keys, values)


def combine_kernel(groups, q_ref, k_ref, v_ref, g_ref, got_ref, stat_ref, att_ref, dq_ref, row_ref):
    head = pl.program_id(0)
    q, k, v, g = q_ref[...], k_ref[...], v_ref[...], g_ref[...]
    key_at = lax.broadcasted_iota(jnp.int32, (BLOCK, BLOCK), 0)
    query_at = lax.broadcasted_iota(jnp.int32, (BLOCK, BLOCK), 1)
    counted = key_at <= query_at
    s = dot_last(k, q) * (SCALE * LOG2E)
    s = jnp.where(counted, s, LOWEST)
    peak = jnp.max(s, axis=0, keepdims=True)
    got_peak = [stat_ref[i, 0, pl.ds(head, 1), :] for i in range(groups)]
    got_norm = [stat_ref[i, 1, pl.ds(head, 1), :] for i in range(groups)]
    peak = functools.reduce(jnp.maximum, got_peak, peak)
    w = jnp.where(counted, jnp.exp2(s - peak), 0.0)
    norm = jnp.sum(w, axis=0, keepdims=True)
    mixed = dot_plain(v.T, w.astype(BF16))
    for i in range(groups):
        factor = jnp.exp2(got_peak[i] - peak)
        norm = norm + got_norm[i] * factor
        mixed = mixed + got_ref[i, 0].astype(F32) * factor
    attention = (mixed / norm).astype(BF16)
    att_ref[...] = attention.T
    lse = peak + jnp.log2(norm)
    delta = jnp.sum(g.T.astype(F32) * attention.astype(F32), axis=0, keepdims=True)
    row_ref[0, pl.ds(head, 1), :] = lse
    row_ref[1, pl.ds(head, 1), :] = delta
    prob = jnp.where(counted, jnp.exp2(s - lse), 0.0)
    ds = (prob * (dot_last(v, g) - delta)).astype(BF16)
    dq_ref[...] = dot_plain(k.T, ds).T * SCALE


def combine(query, keys, values, grad, got, stats):
    rows, width = query.shape
    heads, groups = width // HS, got.shape[0]
    column = pl.BlockSpec((rows, HS), lambda h: (0, h))
    return pl.pallas_call(
        functools.partial(combine_kernel, groups),
        grid=(heads,),
        in_specs=[
            column, column, column, column,
            pl.BlockSpec((groups, 1, HS, BLOCK), lambda h: (0, h, 0, 0)),
            pl.BlockSpec((groups, 2, STAT_ROWS, BLOCK), lambda h: (0, 0, 0, 0)),
        ],
        out_specs=[column, column, pl.BlockSpec((2, STAT_ROWS, BLOCK), lambda h: (0, 0, 0))],
        out_shape=[
            jax.ShapeDtypeStruct((rows, width), BF16),
            jax.ShapeDtypeStruct((rows, width), F32),
            jax.ShapeDtypeStruct((2, STAT_ROWS, BLOCK), F32),
        ],
        compiler_params=pltpu.CompilerParams(vmem_limit_bytes=VMEM_LIMIT),
        cost_estimate=pl.CostEstimate(flops=10**8, bytes_accessed=6 * 10**6, transcendentals=0),
    )(query, keys, values, grad, got, stats)


def backward_kernel(
    blocks, capacity, stored,
    slots_ref, q_ref, g_ref, k_ref, v_ref, row_ref, dq_ref, dk_ref, dv_ref, kt_ref, dka_ref, dva_ref,
):
    head = pl.program_id(0)
    dka_ref[...] = jnp.zeros_like(dka_ref)
    dva_ref[...] = jnp.zeros_like(dva_ref)
    for m in range(stored):
        kt_ref[m] = k_ref[m * BLOCK : (m + 1) * BLOCK, :].T

    def one_block(b, carry):
        count = slots_ref[b, capacity]
        here = pl.ds(pl.multiple_of(b * BLOCK, BLOCK), BLOCK)
        q, g = q_ref[here, :], g_ref[here, :]
        lse = row_ref[b, 0, pl.ds(head, 1), :]
        delta = row_ref[b, 1, pl.ds(head, 1), :]

        def body(n):
            probs, grads = [], []
            total = None
            for j in range(n):
                at = pl.ds(pl.multiple_of(slots_ref[b, j] * BLOCK, BLOCK), BLOCK)
                s = dot_last(k_ref[at, :], q) * (SCALE * LOG2E)
                s = jnp.where(j < count, s, LOWEST)
                prob = jnp.exp2(s - lse)
                ds = (prob * (dot_last(v_ref[at, :], g) - delta)).astype(BF16)
                probs.append(prob.astype(BF16))
                grads.append(ds)
                term = dot_plain(kt_ref[slots_ref[b, j]], ds)
                total = term if total is None else total + term
            dks = [dot_plain(ds, q) for ds in grads]
            dvs = [dot_plain(p, g) for p in probs]
            dq_ref[here, :] = (total * SCALE).T.astype(BF16)
            for j in range(n):
                slot = slots_ref[b, j]
                dka_ref[slot] += dks[j]
                dva_ref[slot] += dvs[j]

        by_count(count, capacity, body)
        return carry

    lax.fori_loop(0, blocks, one_block, 0)
    for m in range(stored):
        dk_ref[m * BLOCK : (m + 1) * BLOCK, :] = (dka_ref[m] * SCALE).astype(BF16)
        dv_ref[m * BLOCK : (m + 1) * BLOCK, :] = dva_ref[m].astype(BF16)


def holder_backward(slots, q_all, g_all, keys, values, row_stats, capacity):
    rows, width = q_all.shape
    heads, blocks, stored = width // HS, rows // BLOCK, keys.shape[0] // BLOCK
    column = lambda n: pl.BlockSpec((n, HS), lambda h, s: (0, h))
    mem = stored * BLOCK
    return pl.pallas_call(
        functools.partial(backward_kernel, blocks, capacity, stored),
        grid_spec=pltpu.PrefetchScalarGridSpec(
            num_scalar_prefetch=1,
            grid=(heads,),
            in_specs=[
                column(rows), column(rows), column(mem), column(mem),
                pl.BlockSpec((blocks, 2, STAT_ROWS, BLOCK), lambda h, s: (0, 0, 0, 0)),
            ],
            out_specs=[column(rows), column(mem), column(mem)],
            scratch_shapes=[
                pltpu.VMEM((stored, HS, BLOCK), BF16),
                pltpu.VMEM((stored, BLOCK, HS), F32),
                pltpu.VMEM((stored, BLOCK, HS), F32),
            ],
        ),
        out_shape=[
            jax.ShapeDtypeStruct((rows, width), BF16),
            jax.ShapeDtypeStruct((mem, width), BF16),
            jax.ShapeDtypeStruct((mem, width), BF16),
        ],
        compiler_params=pltpu.CompilerParams(vmem_limit_bytes=VMEM_LIMIT),
        cost_estimate=pl.CostEstimate(flops=10**10, bytes_accessed=28 * 10**6, transcendentals=0),
    )(slots, q_all, g_all, keys, values, row_stats)


def per_device(
    query, local_keys, local_values, mem_keys, mem_values, block_ids, out_proj, grad_out
):
    groups = lax.axis_size("mem")
    holder = lax.axis_index("mem")
    stored = mem_keys.shape[0] // BLOCK
    capacity = R // groups + 2
    ids = lax.all_gather(block_ids, "mem", axis=0, tiled=True)
    q_all = lax.all_gather(query, "mem", axis=0, tiled=True)
    slots = owned_slots(ids, holder, capacity, stored)
    grad = lax.dot_general(
        lax.all_gather(grad_out, "head", axis=1, tiled=True),
        out_proj,
        (((1,), (1,)), ((), ())),
        preferred_element_type=F32,
    ).astype(BF16)
    g_all = lax.all_gather(grad, "mem", axis=0, tiled=True)
    part, stats = holder_forward(slots, q_all, mem_keys, mem_values, capacity)
    got = lax.all_to_all(part, "mem", split_axis=0, concat_axis=0, tiled=True)
    got_stats = lax.all_to_all(stats, "mem", split_axis=0, concat_axis=0, tiled=True)
    attention, local_dq, row_stats = combine(
        query, local_keys, local_values, grad, got, got_stats
    )
    all_stats = lax.all_gather(row_stats, "mem", axis=0, tiled=False)
    projected = jnp.dot(attention, out_proj, preferred_element_type=F32).astype(BF16)
    output = lax.psum_scatter(projected, "head", scatter_dimension=1, tiled=True)
    dq, grad_mem_keys, grad_mem_values = holder_backward(
        slots, q_all, g_all, mem_keys, mem_values, all_stats, capacity
    )
    mine = lax.psum_scatter(dq, "mem", scatter_dimension=0, tiled=True)
    grad_query = (mine.astype(F32) + local_dq).astype(BF16)
    return (output, grad_query, grad_mem_keys, grad_mem_values)


def solution(mesh):
    split = P("mem", "head")
    placed = (split, split, split, split, split, P("mem", None), P("head", None), split)
    return jax.shard_map(
        per_device, mesh=mesh, in_specs=placed, out_specs=(split,) * 4, check_vma=False
    )
```

time: 892 us -> 429 us (0.48); the launches traced: 880 us -> 430 us
  local copies, waits for them, and re-layouts: 280 us -> 2.56 us
  other arithmetic: 197 us -> 2.93 us
  blocking collectives: 199 us -> 66.4 us
  waiting for transfers between devices: 62.8 us -> 193 us
  Pallas kernels: 0 us -> 129 us
  matrix products: 119 us -> 18.3 us
    scatter-add x16 -> x0, other arithmetic: 155 us -> none  [the longest x8 77.7 us: owner_backward(): value_grad.at[:, slots]]
    gather x64 -> x0, local copies, waits for them, and re-layouts: 134 us -> none  [the longest x32 67.5 us: select(): value_store[:, slots].reshape(local_heads, capacity * BLOCK, HS)]
    pallas_call x0 -> x3, Pallas kernels: none -> 129 us  [the longest x1 73.7 us: holder_backward(): pl.pallas_call(functools.partial(backward_kernel, blocks, capacity, store...]
    all_gather x3 -> x2, blocking collectives: 181 us -> 55 us  [the longest x1 32.7 us: per_device(): all_stats = lax.all_gather(row_stats, 'mem', axis=0, tiled=False)]
    dot_general x60 -> x1, matrix products: 109 us -> 8 us  [per_device(): jnp.dot(attention, out_proj, preferred_element_type=F32).astype(BF16)]
    all_to_all x1, waiting for transfers between devices: 0.01 us -> 70.9 us  [per_device(): got = lax.all_to_all(part, 'mem', split_axis=0, concat_axis=0, tiled=True)]
    unnamed x44 -> x6, local copies, waits for them, and re-layouts: 56.7 us -> 2.39 us
    reduce_scatter x2, waiting for transfers between devices: 41.7 us -> 85.6 us  [the longest x1 58.9 us: per_device(): mine = lax.psum_scatter(dq, 'mem', scatter_dimension=0, tiled=True)]
  transfers between devices with their start and end apart: 6 -> 6, of which waited for: 3 -> 4; matrix products, arithmetic and copies ran while one was open for 13% -> 5% of each run, Pallas kernels for 0% -> 13%
where the time goes in v1:
time: 429 us; the launch traced here: 430 us
  waiting for transfers between devices  193 us (45%)
  Pallas kernels  129 us (30%)
  blocking collectives  66.4 us (15%)
  matrix products  18.3 us (4%)
  between operations  13.8 us (3%)
    pallas_call x1, Pallas kernels, holder_backward(): pl.pallas_call(functools.partial(backward_kernel, blocks, capacity, store...  73.7 us
    all_to_all x1, waiting for transfers between devices, per_device(): got = lax.all_to_all(part, 'mem', split_axis=0, concat_axis=0, tiled=True)  70.9 us
    reduce_scatter x1, waiting for transfers between devices, per_device(): mine = lax.psum_scatter(dq, 'mem', scatter_dimension=0, tiled=True)  58.9 us
    pallas_call x1, Pallas kernels, holder_forward(): pl.pallas_call(functools.partial(forward_kernel, blocks, capacity, stored...  45.4 us
    all_gather x1, waiting for transfers between devices, per_device(): q_all = lax.all_gather(query, 'mem', axis=0, tiled=True)  35.3 us
    all_gather x1, blocking collectives, per_device(): all_stats = lax.all_gather(row_stats, 'mem', axis=0, tiled=False)  32.7 us
    reduce_scatter x1, waiting for transfers between devices, per_device(): lax.psum_scatter(projected, 'head', scatter_dimension=1, tiled=True)  26.7 us
    all_gather x1, blocking collectives, per_device(): ids = lax.all_gather(block_ids, 'mem', axis=0, tiled=True)  22.3 us
  transfers between devices with their start and end apart: 6, of which 4 were waited for; matrix products, arithmetic and copies ran while one was open for 5% of the time, Pallas kernels for 13%

profile of v1, /device:TPU:0, one launch (start us, length us, event | category | flops | bytes accessed | tf_op | source)
XLA Modules:
  0.0 429.9 jit_solution(12119406073988659037)
XLA Ops:
  7.2 0.0 all-gather.8.cloned.1.call-start
  7.2 0.7 all-gather.8.cloned.1.call-update
  7.9 0.0 all-gather.6.cloned.1.call-start
  7.9 0.7 all-gather.6.cloned.1.call-update
  8.7 22.3 %all-gather.1 = s32[8,1,32]{2,1,0:T(1,128)S(1)} all-gather(s32[1,1,32]{2,1,0:T(1,128)} %bitcast.11), channel_id=1, replica_groups=mesh['mem'=8,'head'=4] {'mem'}, dimensions={0}, use_global_device_ids=true | all-gather | bytes 1152 | tf_op jit(solution)/shard_map/all_gather | solution.py:250
  31.0 0.2 reduce_window_sum.11
  31.2 0.2 select_reduce_fusion
  31.3 0.1 copy.15
  31.4 0.1 convert_reduce_fusion
  31.5 0.1 copy.16
  31.6 0.7 pad_add_fusion.slots_ref
  32.3 35.3 %all-gather.8.cloned.1.call-done.q_ref = bf16[1024,1280]{1,0:T(8,128)(2,1)} async-done(((bf16[128,1280]{1,0:T(8,128)(2,1)}), bf16[1024,1280]{1,0:T(8,128)(2,1)}) %all-gather.8.cloned.1.call-update) | async-done | bytes 2621456 | tf_op jit(solution)/shard_map/all_gather | solution.py:251
  67.6 45.4 %shard_map.111 = (bf16[8,10,128,128]{3,2,1,0:T(8,128)(2,1)}, f32[8,2,16,128]{3,2,1,0:T(8,128)}) custom-call(s32[8,7]{1,0:T(8,128)} %pad_add_fusion.slots_ref, bf16[1024,1280]{1,0:T(8,128)(2,1)} %all-gather.8.cloned.1.call-done.q_ref, bf16[2048,1280]{1,0:T(8,128)(2,1)} %k_ref.5, bf16[2048,1280]{1,0:T(8,128)(2,1)} %v_ref.5), custom_call_target="tpu_custom_call" | custom-call | flops 4000000000 | bytes 16000000 | tf_op jit(solution)/shard_map/pallas_call | solution.py:91
  113.0 11.3 %all_to_all.10.stat_ref = f32[8,2,16,128]{3,2,1,0:T(8,128)} all-to-all(f32[8,2,16,128]{3,2,1,0:T(8,128)} %get-tuple-element.13), channel_id=1, replica_groups=mesh['mem'=8,'head'=4] {'mem'}, dimensions={0} | all-to-all | bytes 262144 | tf_op jit(solution)/shard_map/all_to_all | solution.py:262
  124.4 3.6 all-to-all-start
  128.0 0.0 all-gather.10.cloned.1.call-start
  128.0 0.0 all-gather.6.cloned.1.call-done
  128.1 10.3 %convolution_convert_fusion.1.g_ref = bf16[128,1280]{1,0:T(8,128)(2,1)} fusion(bf16[128,5120]{1,0:T(8,128)(2,1)} %all-gather.6.cloned.1.call-done, bf16[1280,5120]{1,0:T(8,128)(2,1)} %param.14), kind=kOutput, calls=%fused_computation.1 | convolution fusion | flops 1677885440 | bytes 14745600 | tf_op jit(solution)/shard_map/dot_general | solution.py:253
  138.3 0.0 all-gather.10.cloned.1.call-update
  138.4 0.0 reduce-scatter.5.cloned.1.call-start
  138.4 70.9 %all-to-all-done.got_ref = bf16[8,10,128,128]{3,2,1,0:T(8,128)(2,1)S(1)} async-done(((bf16[8,10,128,128]{3,2,1,0:T(8,128)(2,1)}), bf16[8,10,128,128]{3,2,1,0:T(8,128)(2,1)S(1)}, u32[]{:S(2)}, u32[]{:S(2)}) %all-to-all-start) | async-done | bytes 2621472 | tf_op jit(solution)/shard_map/all_to_all | solution.py:261
  209.3 0.0 copy-start
  209.3 1.5 copy-done
  210.8 9.8 %shard_map.112 = (bf16[128,1280]{1,0:T(8,128)(2,1)}, f32[128,1280]{1,0:T(8,128)}, f32[2,16,128]{2,1,0:T(8,128)}) custom-call(bf16[128,1280]{1,0:T(8,128)(2,1)} %q_ref.1, bf16[128,1280]{1,0:T(8,128)(2,1)} %k_ref.4, bf16[128,1280]{1,0:T(8,128)(2,1)} %v_ref.4, bf16[128,1280]{1,0:T(8,128)(2,1)} %convolution_convert_fusion.1.g_ref, ...), custom_call_target="tpu_custom_call" | custom-call | flops 100000000 | bytes 6000000 | tf_op jit(solution)/shard_map/pallas_call | solution.py:146
  220.6 32.7 %all-gather = f32[16,16,128]{2,1,0:T(8,128)} all-gather(f32[2,16,128]{2,1,0:T(8,128)} %get-tuple-element.15), channel_id=2, replica_groups=mesh['mem'=8,'head'=4] {'mem'}, dimensions={0}, use_global_device_ids=true | all-gather | bytes 147456 | tf_op jit(solution)/shard_map/all_gather | solution.py:266
  253.3 0.0 all-gather.10.cloned.1.call-done.g_ref
  253.3 73.7 %shard_map.113 = (bf16[1024,1280]{1,0:T(8,128)(2,1)}, bf16[2048,1280]{1,0:T(8,128)(2,1)}, bf16[2048,1280]{1,0:T(8,128)(2,1)}) custom-call(s32[8,7]{1,0:T(8,128)} %pad_add_fusion.slots_ref, bf16[1024,1280]{1,0:T(8,128)(2,1)} %all-gather.8.cloned.1.call-done.q_ref, bf16[1024,1280]{1,0:T(8,128)(2,1)} %all-gather.10.cloned.1.call-done.g_ref, ...), custom_call_target="tpu_custom_call" | custom-call | flops 10000000000 | bytes 28000000 | tf_op jit(solution)/shard_map/pallas_call | solution.py:217
  327.0 0.0 copy-start.2
  327.0 0.0 reduce-scatter.5.cloned.1.call-update
  327.1 0.0 reduce-scatter.3.cloned.1.call-start
  327.1 0.9 copy-done.2
  328.0 0.0 copy-start.1
  328.0 8.0 %convolution_convert_fusion = bf16[128,5120]{1,0:T(8,128)(2,1)} fusion(bf16[128,1280]{1,0:T(8,128)(2,1)S(1)} %copy-done.2, bf16[1280,5120]{1,0:T(8,128)(2,1)} %param.14), kind=kOutput, calls=%fused_computation | convolution fusion | flops 1678376960 | bytes 14745600 | tf_op jit(solution)/shard_map/dot_general | solution.py:267
  336.0 0.0 reduce-scatter.3.cloned.1.call-update
  336.0 58.9 %reduce-scatter.5.cloned.1.call-done = bf16[128,1280]{1,0:T(8,128)(2,1)} async-done(((bf16[1024,1280]{1,0:T(8,128)(2,1)}), bf16[128,1280]{1,0:T(8,128)(2,1)}) %reduce-scatter.5.cloned.1.call-update) | async-done | bytes 327696 | tf_op jit(solution)/shard_map/reduce_scatter | solution.py:272
  395.0 0.0 copy-done.1
  395.0 1.8 add_convert_fusion
  396.7 26.7 %reduce-scatter.3.cloned.1.call-done = bf16[128,1280]{1,0:T(8,128)(2,1)} async-done(((bf16[128,5120]{1,0:T(8,128)(2,1)}), bf16[128,1280]{1,0:T(8,128)(2,1)}) %reduce-scatter.3.cloned.1.call-update) | async-done | bytes 327696 | tf_op jit(solution)/shard_map/reduce_scatter | solution.py:268
  (2 shorter events, 0.0 us)
Async XLA Ops:
  7.2 60.4 %all-gather.8.cloned.1.call-start = ((), (), s32[]{:S(2)}) async-start(), calls=%async_computation.5 | async-start | bytes 2949120 | tf_op jit(solution)/shard_map/all_gather | solution.py:251
  7.9 120.2 %all-gather.6.cloned.1.call-start = ((), (), s32[]{:S(2)}) async-start(), calls=%async_computation.4 | async-start | bytes 1638400 | tf_op jit(solution)/shard_map/all_gather | solution.py:254
  124.4 84.9 %all-to-all-start = ((bf16[8,10,128,128]{3,2,1,0:T(8,128)(2,1)}), bf16[8,10,128,128]{3,2,1,0:T(8,128)(2,1)S(1)}, u32[]{:S(2)}, u32[]{:S(2)}) async-start(bf16[8,10,128,128]{3,2,1,0:T(8,128)(2,1)} %get-tuple-element.12), calls=%async_computation | async-start | bytes 5242880 | tf_op jit(solution)/shard_map/all_to_all | solution.py:261
  128.0 125.3 %all-gather.10.cloned.1.call-start = ((), (), s32[]{:S(2)}) async-start(), calls=%async_computation.7 | async-start | bytes 2949120 | tf_op jit(solution)/shard_map/all_gather | solution.py:259
  138.4 256.6 %reduce-scatter.5.cloned.1.call-start = ((), (), s32[]{:S(2)}) async-start(), calls=%async_computation.8 | async-start | bytes 2949120 | tf_op jit(solution)/shard_map/reduce_scatter | solution.py:272
  209.3 1.5 copy-start
  327.0 1.0 copy-start.2
  327.1 96.4 %reduce-scatter.3.cloned.1.call-start = ((), (), s32[]{:S(2)}) async-start(), calls=%async_computation.6 | async-start | bytes 1638400 | tf_op jit(solution)/shard_map/reduce_scatter | solution.py:268
  328.0 67.0 %copy-start.1 = (f32[128,1280]{1,0:T(8,128)S(1)}, f32[128,1280]{1,0:T(8,128)}, u32[]{:S(2)}) copy-start(f32[128,1280]{1,0:T(8,128)} %get-tuple-element.17) | copy-start | bytes 1966084
Sparse Core Ops, SparseCore 0:
  10.2 57.3 all-gather.7
  69.2 17.0 all-gather.5
  138.5 78.9 all-gather.9
  327.2 67.7 reduce-scatter.4
  397.9 25.4 reduce-scatter.2

commit v2 on v1

v2 whole, which is shorter than its diff:
```python
import functools
import math

import jax
import jax.numpy as jnp
from jax import lax
from jax.experimental import pallas as pl
from jax.experimental.pallas import tpu as pltpu
from jax.sharding import PartitionSpec as P

HS = 128
BLOCK = 128
R = 32
STAT_ROWS = 16
LOWEST = -1e30
SCALE = HS ** (-0.5)
LOG2E = math.log2(math.e)
F32 = jnp.float32
BF16 = jnp.bfloat16
MESH = pl.DeviceIdType.MESH
VMEM_LIMIT = 56 * 1024 * 1024


def dot_last(a, b):
    return lax.dot_general(a, b, (((1,), (1,)), ((), ())), preferred_element_type=F32)


def dot_plain(a, b):
    return lax.dot_general(a, b, (((1,), (0,)), ((), ())), preferred_element_type=F32)


def owned_slots(ids, holder, capacity, stored):
    is_owned = ids // stored == holder
    rank = jnp.cumsum(is_owned.astype(jnp.int32), axis=1) - 1
    chosen = jnp.logical_and(
        is_owned[:, None, :], rank[:, None, :] == jnp.arange(capacity, dtype=jnp.int32)[None, :, None]
    )
    slots = jnp.sum(jnp.where(chosen, (ids % stored)[:, None, :], 0), axis=2).astype(jnp.int32)
    count = jnp.sum(is_owned.astype(jnp.int32), axis=1, keepdims=True)
    return jnp.concatenate([slots, count], axis=1)


def meet(groups, me):
    barrier = pltpu.get_barrier_semaphore()
    for d in range(1, groups):
        pl.semaphore_signal(
            barrier, inc=1, device_id={"mem": lax.rem(me + d, groups)}, device_id_type=MESH
        )
    pl.semaphore_wait(barrier, groups - 1)


def push(src, dst, send_sem, recv_sem, peer):
    return pltpu.make_async_remote_copy(
        src_ref=src,
        dst_ref=dst,
        send_sem=send_sem,
        recv_sem=recv_sem,
        device_id={"mem": peer},
        device_id_type=MESH,
    )


def remote_params(collective_id):
    return pltpu.CompilerParams(
        vmem_limit_bytes=VMEM_LIMIT, collective_id=collective_id, has_side_effects=True
    )


def ring_kernel(groups, x_ref, i_ref, xs_ref, is_ref, local, xsend, xrecv, isend, irecv):
    me = lax.axis_index("mem")
    place = (1 - me % 2) * (me // 2) + (me % 2) * (groups - 1 - me // 2)

    def device_at(p):
        p = lax.rem(p + groups, groups)
        upper = p // (groups // 2)
        return (1 - upper) * (2 * p) + upper * (2 * (groups - 1 - p) + 1)

    sides = (device_at(place + 1), device_at(place - 1))
    barrier = pltpu.get_barrier_semaphore()
    for side in sides:
        pl.semaphore_signal(barrier, inc=1, device_id={"mem": side}, device_id_type=MESH)
    pl.semaphore_wait(barrier, 2)
    own = [
        pltpu.make_async_copy(x_ref, xs_ref.at[me], local.at[0]),
        pltpu.make_async_copy(i_ref, is_ref.at[me], local.at[1]),
    ]
    for copy in own:
        copy.start()
    steps = (groups // 2, groups - 1 - groups // 2)
    sent = []
    for t in range(steps[0]):
        for way in range(2):
            if t >= steps[way]:
                continue
            sign = 1 - 2 * way
            block = device_at(place - sign * t)
            if t:
                before = device_at(place - sign * t)
                push(x_ref, xs_ref.at[before], xsend.at[way, t - 1], xrecv.at[way, t - 1], sides[way]).wait_recv()
                push(i_ref, is_ref.at[before], isend.at[way, t - 1], irecv.at[way, t - 1], sides[way]).wait_recv()
            for src, dst, ss, rs in (
                (x_ref if t == 0 else xs_ref.at[block], xs_ref.at[block], xsend, xrecv),
                (i_ref if t == 0 else is_ref.at[block], is_ref.at[block], isend, irecv),
            ):
                copy = push(src, dst, ss.at[way, t], rs.at[way, t], sides[way])
                copy.start()
                sent.append(copy)
    for way in range(2):
        t = steps[way]
        last = device_at(place - (1 - 2 * way) * t)
        push(x_ref, xs_ref.at[last], xsend.at[way, t - 1], xrecv.at[way, t - 1], sides[way]).wait_recv()
        push(i_ref, is_ref.at[last], isend.at[way, t - 1], irecv.at[way, t - 1], sides[way]).wait_recv()
    for copy in sent:
        copy.wait_send()
    for copy in own:
        copy.wait()


def ring_gather(x, ids, groups):
    steps = groups // 2
    anywhere = pl.BlockSpec(memory_space=pl.ANY)
    return pl.pallas_call(
        functools.partial(ring_kernel, groups),
        in_specs=[anywhere, anywhere],
        out_specs=[anywhere, anywhere],
        out_shape=[
            jax.ShapeDtypeStruct((groups,) + x.shape, x.dtype),
            jax.ShapeDtypeStruct((groups,) + ids.shape, ids.dtype),
        ],
        scratch_shapes=[pltpu.SemaphoreType.DMA((2,))] + [pltpu.SemaphoreType.DMA((2, steps))] * 4,
        compiler_params=remote_params(0),
    )(x, ids)


def forward_kernel(
    groups, heads, capacity, stored,
    slots_ref, mask_ref, q_ref, k_ref, v_ref, got_ref, gstat_ref,
    vt_ref, part_ref, stat_ref, send, recv, ssend, srecv, local,
):
    head = pl.program_id(0)
    me = lax.axis_index("mem")

    @pl.when(head == 0)
    def _():
        meet(groups, me)
        stat_ref[...] = jnp.zeros_like(stat_ref)

    for m in range(stored):
        vt_ref[m] = v_ref[m].T

    def one_block(b, carry):
        q = q_ref[pl.ds(pl.multiple_of(b * BLOCK, BLOCK), BLOCK), :]
        scores = []
        for j in range(capacity):
            s = dot_last(k_ref[slots_ref[b, j]], q) * (SCALE * LOG2E)
            scores.append(s + mask_ref[b, j : j + 1, :])
        peak = jnp.max(functools.reduce(jnp.maximum, scores), axis=0, keepdims=True)
        weights = [jnp.exp2(s - peak) for s in scores]
        norm = jnp.sum(functools.reduce(jnp.add, weights), axis=0, keepdims=True)
        total = None
        for j in range(capacity):
            term = dot_plain(vt_ref[slots_ref[b, j]], weights[j].astype(BF16))
            total = term if total is None else total + term
        part_ref[head, b] = total.astype(BF16)
        stat_ref[b, 0, pl.ds(head, 1), :] = peak
        stat_ref[b, 1, pl.ds(head, 1), :] = norm
        return carry

    lax.fori_loop(0, groups, one_block, 0)

    def part_push(h, peer, owner):
        return push(
            part_ref.at[h, peer], got_ref.at[owner, h], send.at[h, peer], recv.at[h, owner], peer
        )

    def part_keep(h):
        return pltpu.make_async_copy(part_ref.at[h, me], got_ref.at[me, h], local.at[h])

    def stat_push(peer, owner):
        return push(
            stat_ref.at[peer], gstat_ref.at[owner], ssend.at[peer], srecv.at[owner], peer
        )

    for d in range(1, groups):
        part_push(head, lax.rem(me + d, groups), me).start()
    part_keep(head).start()

    @pl.when(head == heads - 1)
    def _():
        keep = pltpu.make_async_copy(stat_ref.at[me], gstat_ref.at[me], local.at[heads])
        keep.start()
        for d in range(1, groups):
            stat_push(lax.rem(me + d, groups), me).start()

        def finish(h, carry):
            for d in range(1, groups):
                peer = lax.rem(me + d, groups)
                part_push(h, peer, me).wait_send()
                part_push(h, peer, peer).wait_recv()
            part_keep(h).wait()
            return carry

        lax.fori_loop(0, heads, finish, 0)
        for d in range(1, groups):
            peer = lax.rem(me + d, groups)
            stat_push(peer, me).wait_send()
            stat_push(peer, peer).wait_recv()
        keep.wait()


def holder_forward(slots, mask, q_all, keys, values, capacity):
    rows, width = q_all.shape
    heads, groups, stored = width // HS, rows // BLOCK, keys.shape[0]
    column = lambda n: pl.BlockSpec((n, HS), lambda h: (0, h))
    store = pl.BlockSpec((stored, BLOCK, HS), lambda h: (0, 0, h))
    fixed = lambda shape: pl.BlockSpec(shape, lambda h: (0,) * len(shape))
    anywhere = pl.BlockSpec(memory_space=pl.ANY)
    dma = pltpu.SemaphoreType.DMA
    return pl.pallas_call(
        functools.partial(forward_kernel, groups, heads, capacity, stored),
        grid=(heads,),
        in_specs=[
            pl.BlockSpec(memory_space=pltpu.SMEM),
            fixed(mask.shape), column(rows), store, store,
        ],
        out_specs=[anywhere, anywhere],
        scratch_shapes=[
            pltpu.VMEM((stored, HS, BLOCK), BF16),
            pltpu.VMEM((heads, groups, HS, BLOCK), BF16),
            pltpu.VMEM((groups, 2, STAT_ROWS, BLOCK), F32),
            dma((heads, groups)), dma((heads, groups)), dma((groups,)), dma((groups,)),
            dma((heads + 1,)),
        ],
        out_shape=[
            jax.ShapeDtypeStruct((groups, heads, HS, BLOCK), BF16),
            jax.ShapeDtypeStruct((groups, 2, STAT_ROWS, BLOCK), F32),
        ],
        compiler_params=remote_params(1),
        cost_estimate=pl.CostEstimate(flops=4 * 10**9, bytes_accessed=16 * 10**6, transcendentals=0),
    )(slots, mask, q_all, keys, values)


def combine_kernel(
    groups, heads, q_ref, k_ref, v_ref, g_ref, got_ref, stat_ref, att_ref, dq_ref, all_ref,
    row_ref, send, recv, local,
):
    head = pl.program_id(0)
    me = lax.axis_index("mem")

    @pl.when(head == 0)
    def _():
        meet(groups, me)
        row_ref[...] = jnp.zeros_like(row_ref)

    q, k, v, g = q_ref[...], k_ref[...], v_ref[...], g_ref[...]
    key_at = lax.broadcasted_iota(jnp.int32, (BLOCK, BLOCK), 0)
    query_at = lax.broadcasted_iota(jnp.int32, (BLOCK, BLOCK), 1)
    counted = key_at <= query_at
    s = dot_last(k, q) * (SCALE * LOG2E)
    s = jnp.where(counted, s, LOWEST)
    peak = jnp.max(s, axis=0, keepdims=True)
    got_peak = [stat_ref[i, 0, pl.ds(head, 1), :] for i in range(groups)]
    got_norm = [stat_ref[i, 1, pl.ds(head, 1), :] for i in range(groups)]
    peak = functools.reduce(jnp.maximum, got_peak, peak)
    w = jnp.where(counted, jnp.exp2(s - peak), 0.0)
    norm = jnp.sum(w, axis=0, keepdims=True)
    mixed = dot_plain(v.T, w.astype(BF16))
    for i in range(groups):
        factor = jnp.exp2(got_peak[i] - peak)
        norm = norm + got_norm[i] * factor
        mixed = mixed + got_ref[i, 0].astype(F32) * factor
    attention = (mixed / norm).astype(BF16)
    att_ref[...] = attention.T
    lse = peak + jnp.log2(norm)
    delta = jnp.sum(g.T.astype(F32) * attention.astype(F32), axis=0, keepdims=True)
    row_ref[0, pl.ds(head, 1), :] = lse
    row_ref[1, pl.ds(head, 1), :] = delta
    prob = jnp.where(counted, jnp.exp2(s - lse), 0.0)
    ds = (prob * (dot_last(v, g) - delta)).astype(BF16)
    dq_ref[...] = dot_plain(k.T, ds).T * SCALE

    @pl.when(head == heads - 1)
    def _():
        keep = pltpu.make_async_copy(row_ref, all_ref.at[me], local.at[0])
        keep.start()

        def row_push(peer, owner):
            return push(row_ref, all_ref.at[owner], send.at[peer], recv.at[owner], peer)

        for d in range(1, groups):
            row_push(lax.rem(me + d, groups), me).start()
        for d in range(1, groups):
            peer = lax.rem(me + d, groups)
            row_push(peer, me).wait_send()
            row_push(peer, peer).wait_recv()
        keep.wait()


def combine(query, keys, values, grad, got, stats):
    rows, width = query.shape
    heads, groups = width // HS, got.shape[0]
    column = pl.BlockSpec((rows, HS), lambda h: (0, h))
    dma = pltpu.SemaphoreType.DMA
    return pl.pallas_call(
        functools.partial(combine_kernel, groups, heads),
        grid=(heads,),
        in_specs=[
            column, column, column, column,
            pl.BlockSpec((groups, 1, HS, BLOCK), lambda h: (0, h, 0, 0)),
            pl.BlockSpec((groups, 2, STAT_ROWS, BLOCK), lambda h: (0, 0, 0, 0)),
        ],
        out_specs=[column, column, pl.BlockSpec(memory_space=pl.ANY)],
        out_shape=[
            jax.ShapeDtypeStruct((rows, width), BF16),
            jax.ShapeDtypeStruct((rows, width), F32),
            jax.ShapeDtypeStruct((groups, 2, STAT_ROWS, BLOCK), F32),
        ],
        scratch_shapes=[
            pltpu.VMEM((2, STAT_ROWS, BLOCK), F32), dma((groups,)), dma((groups,)), dma((1,)),
        ],
        compiler_params=remote_params(2),
        cost_estimate=pl.CostEstimate(flops=10**8, bytes_accessed=6 * 10**6, transcendentals=0),
    )(query, keys, values, grad, got, stats)


def backward_kernel(
    groups, heads, capacity, stored,
    slots_ref, terms_ref, mask_ref, q_ref, g_ref, k_ref, v_ref, row_ref, got_ref, dk_ref, dv_ref,
    kt_ref, dkp_ref, dvp_ref, part_ref, send, recv, local,
):
    head = pl.program_id(0)
    me = lax.axis_index("mem")

    @pl.when(head == 0)
    def _():
        meet(groups, me)
        dkp_ref[groups * capacity] = jnp.zeros((BLOCK, HS), F32)
        dvp_ref[groups * capacity] = jnp.zeros((BLOCK, HS), F32)

    for m in range(stored):
        kt_ref[m] = k_ref[m].T

    def one_block(b, carry):
        here = pl.ds(pl.multiple_of(b * BLOCK, BLOCK), BLOCK)
        q, g = q_ref[here, :], g_ref[here, :]
        lse = row_ref[b, 0, pl.ds(head, 1), :]
        delta = row_ref[b, 1, pl.ds(head, 1), :]
        total = None
        for j in range(capacity):
            s = dot_last(k_ref[slots_ref[b, j]], q) * (SCALE * LOG2E)
            s = s + mask_ref[b, j : j + 1, :]
            prob = jnp.exp2(s - lse)
            ds = (prob * (dot_last(v_ref[slots_ref[b, j]], g) - delta)).astype(BF16)
            term = dot_plain(kt_ref[slots_ref[b, j]], ds)
            total = term if total is None else total + term
            dkp_ref[b * capacity + j] = dot_plain(ds, q)
            dvp_ref[b * capacity + j] = dot_plain(prob.astype(BF16), g)
        part_ref[head, b] = (total * SCALE).T.astype(BF16)
        return carry

    lax.fori_loop(0, groups, one_block, 0)

    def part_push(h, peer, owner):
        at = pl.ds(pl.multiple_of(h * HS, HS), HS)
        return push(
            part_ref.at[h, peer], got_ref.at[owner, :, at], send.at[h, peer], recv.at[h, owner], peer
        )

    def part_keep(h):
        at = pl.ds(pl.multiple_of(h * HS, HS), HS)
        return pltpu.make_async_copy(part_ref.at[h, me], got_ref.at[me, :, at], local.at[h])

    for d in range(1, groups):
        part_push(head, lax.rem(me + d, groups), me).start()
    part_keep(head).start()

    def one_slot(m, carry):
        at = pl.ds(pl.multiple_of(m * BLOCK, BLOCK), BLOCK)
        dk = functools.reduce(jnp.add, [dkp_ref[terms_ref[m, b]] for b in range(groups)])
        dv = functools.reduce(jnp.add, [dvp_ref[terms_ref[m, b]] for b in range(groups)])
        dk_ref[at, :] = (dk * SCALE).astype(BF16)
        dv_ref[at, :] = dv.astype(BF16)
        return carry

    lax.fori_loop(0, stored, one_slot, 0)

    @pl.when(head == heads - 1)
    def _():
        def finish(h, carry):
            for d in range(1, groups):
                peer = lax.rem(me + d, groups)
                part_push(h, peer, me).wait_send()
                part_push(h, peer, peer).wait_recv()
            part_keep(h).wait()
            return carry

        lax.fori_loop(0, heads, finish, 0)


def holder_backward(slots, terms, mask, q_all, g_all, keys, values, row_stats, capacity):
    rows, width = q_all.shape
    heads, groups, stored = width // HS, rows // BLOCK, keys.shape[0]
    column = lambda n: pl.BlockSpec((n, HS), lambda h: (0, h))
    store = pl.BlockSpec((stored, BLOCK, HS), lambda h: (0, 0, h))
    fixed = lambda shape: pl.BlockSpec(shape, lambda h: (0,) * len(shape))
    mem = stored * BLOCK
    dma = pltpu.SemaphoreType.DMA
    smem = pl.BlockSpec(memory_space=pltpu.SMEM)
    return pl.pallas_call(
        functools.partial(backward_kernel, groups, heads, capacity, stored),
        grid=(heads,),
        in_specs=[
            smem, smem, fixed(mask.shape), column(rows), column(rows), store, store,
            pl.BlockSpec((groups, 2, STAT_ROWS, BLOCK), lambda h: (0, 0, 0, 0)),
        ],
        out_specs=[pl.BlockSpec(memory_space=pl.ANY), column(mem), column(mem)],
        scratch_shapes=[
            pltpu.VMEM((stored, HS, BLOCK), BF16),
            pltpu.VMEM((groups * capacity + 1, BLOCK, HS), F32),
            pltpu.VMEM((groups * capacity + 1, BLOCK, HS), F32),
            pltpu.VMEM((heads, groups, BLOCK, HS), BF16),
            dma((heads, groups)), dma((heads, groups)), dma((heads,)),
        ],
        out_shape=[
            jax.ShapeDtypeStruct((groups, BLOCK, width), BF16),
            jax.ShapeDtypeStruct((mem, width), BF16),
            jax.ShapeDtypeStruct((mem, width), BF16),
        ],
        compiler_params=remote_params(3),
        cost_estimate=pl.CostEstimate(flops=10**10, bytes_accessed=28 * 10**6, transcendentals=0),
    )(slots, terms, mask, q_all, g_all, keys, values, row_stats)


def slot_terms(slots, capacity, stored):
    blocks = slots.shape[0]
    place = jnp.arange(capacity, dtype=jnp.int32)
    pair = jnp.arange(blocks, dtype=jnp.int32)[:, None] * capacity + place[None, :]
    filled = place[None, :] < slots[:, capacity:]
    match = jnp.logical_and(
        filled[None], slots[None, :, :capacity] == jnp.arange(stored, dtype=jnp.int32)[:, None, None]
    )
    none = blocks * capacity
    return none + jnp.sum(jnp.where(match, pair[None] - none, 0), axis=2).astype(jnp.int32)


def per_device(
    query, local_keys, local_values, mem_keys, mem_values, block_ids, out_proj, grad_out
):
    groups = lax.axis_size("mem")
    holder = lax.axis_index("mem")
    stored = mem_keys.shape[0] // BLOCK
    capacity = R // groups + 2
    width = query.shape[1]
    padded = jnp.pad(block_ids, ((0, 7), (0, HS - R)))
    q_all, ids = ring_gather(query, padded, groups)
    q_all = q_all.reshape(groups * BLOCK, width)
    slots = owned_slots(ids[:, 0, :R], holder, capacity, stored)
    terms = slot_terms(slots, capacity, stored)
    grad = lax.dot_general(
        lax.all_gather(grad_out, "head", axis=1, tiled=True),
        out_proj,
        (((1,), (1,)), ((), ())),
        preferred_element_type=F32,
    ).astype(BF16)
    g_all = lax.all_gather(grad, "mem", axis=0, tiled=True)
    slots, grad = lax.optimization_barrier((slots, grad))
    filled = jnp.arange(capacity, dtype=jnp.int32)[None, :] < slots[:, capacity:]
    mask = jnp.broadcast_to(
        jnp.where(filled, 0.0, LOWEST).astype(F32)[:, :, None], (groups, capacity, BLOCK)
    )
    key_store = mem_keys.reshape(stored, BLOCK, width)
    value_store = mem_values.reshape(stored, BLOCK, width)
    got, got_stats = holder_forward(slots, mask, q_all, key_store, value_store, capacity)
    attention, local_dq, all_stats = combine(
        query, local_keys, local_values, grad, got, got_stats
    )
    projected = jnp.dot(attention, out_proj, preferred_element_type=F32).astype(BF16)
    projected, all_stats = lax.optimization_barrier((projected, all_stats))
    output = lax.psum_scatter(projected, "head", scatter_dimension=1, tiled=True)
    got_dq, grad_mem_keys, grad_mem_values = holder_backward(
        slots, terms, mask, q_all, g_all, key_store, value_store, all_stats, capacity
    )
    grad_query = (jnp.sum(got_dq.astype(F32), axis=0) + local_dq).astype(BF16)
    return (output, grad_query, grad_mem_keys, grad_mem_values)


def solution(mesh):
    split = P("mem", "head")
    placed = (split, split, split, split, split, P("mem", None), P("head", None), split)
    return jax.shard_map(
        per_device, mesh=mesh, in_specs=placed, out_specs=(split,) * 4, check_vma=False
    )
```

time: 429 us -> 352 us (0.82)
  waiting for transfers between devices: 193 us -> 23.3 us
  Pallas kernels: 129 us -> 279 us
  blocking collectives: 66.4 us -> 0 us
  local copies, waits for them, and re-layouts: 2.56 us -> 12.9 us
    pallas_call x3 -> x4, Pallas kernels: 129 us -> 279 us  [the longest x1 131 us: holder_backward(): pl.pallas_call(functools.partial(backward_kernel, groups, heads, capacity...]
    all_to_all x1 -> x0, waiting for transfers between devices: 70.9 us -> none  [per_device(): got = lax.all_to_all(part, 'mem', split_axis=0, concat_axis=0, tiled=True)]
    reduce_scatter x1 -> x0, waiting for transfers between devices: 58.9 us -> none  [per_device(): mine = lax.psum_scatter(dq, 'mem', scatter_dimension=0, tiled=True)]
    all_gather x2 -> x0, blocking collectives: 55 us -> none  [the longest x1 32.7 us: per_device(): all_stats = lax.all_gather(row_stats, 'mem', axis=0, tiled=False)]
    all_gather x1 -> x0, waiting for transfers between devices: 35.3 us -> none  [per_device(): q_all = lax.all_gather(query, 'mem', axis=0, tiled=True)]
    reduce_scatter x1, waiting for transfers between devices: 26.7 us -> 0.01 us  [per_device(): lax.psum_scatter(projected, 'head', scatter_dimension=1, tiled=True)]
    all_gather x1, waiting for transfers between devices: 0.02 us -> 22.5 us  [per_device(): lax.all_gather(grad_out, 'head', axis=1, tiled=True)]
    all_to_all x1 -> x0, blocking collectives: 11.3 us -> none  [per_device(): lax.all_to_all(stats, 'mem', split_axis=0, concat_axis=0, tiled=True)]
  transfers between devices with their start and end apart: 6 -> 3, of which waited for: 4 -> 1; matrix products, arithmetic and copies ran while one was open for 5% -> 4% of each run, Pallas kernels for 13% -> 79%
where the time goes in v2:
time: 352 us
  Pallas kernels  279 us (79%)
  waiting for transfers between devices  23.3 us (7%)
  matrix products  18 us (5%)
  between operations  13.9 us (4%)
  local copies, waits for them, and re-layouts  12.9 us (4%)
  other arithmetic  5.11 us (1%)
    pallas_call x1, Pallas kernels, holder_backward(): pl.pallas_call(functools.partial(backward_kernel, groups, heads, capacity...  131 us
    pallas_call x1, Pallas kernels, holder_forward(): pl.pallas_call(functools.partial(forward_kernel, groups, heads, capacity,...  73.1 us
    pallas_call x1, Pallas kernels, ring_gather(): pl.pallas_call(functools.partial(ring_kernel, groups), in_specs=[anywhere...  57.2 us
    all_gather x1, waiting for transfers between devices, per_device(): lax.all_gather(grad_out, 'head', axis=1, tiled=True)  22.5 us
    pallas_call x1, Pallas kernels, combine(): pl.pallas_call(functools.partial(combine_kernel, groups, heads), grid=(he...  16.8 us
    unnamed x8, local copies, waits for them, and re-layouts  10.4 us
    dot_general x1, matrix products, per_device(): lax.dot_general(lax.all_gather(grad_out, 'head', axis=1, tiled=True), out...  10.3 us
    dot_general x1, matrix products, per_device(): jnp.dot(attention, out_proj, preferred_element_type=F32).astype(BF16)  7.78 us
  transfers between devices with their start and end apart: 3, of which 1 were waited for; matrix products, arithmetic and copies ran while one was open for 4% of the time, Pallas kernels for 79%

profile of v2, /device:TPU:0, one launch (start us, length us, event | category | flops | bytes accessed | tf_op | source)
XLA Modules:
  0.0 351.9 jit_solution(15058273679734293822)
XLA Ops:
  7.2 0.0 all-gather.3.cloned.1.call-start
  7.2 0.7 all-gather.3.cloned.1.call-update
  7.9 0.0 copy-start.2
  7.9 0.0 all-gather.5.cloned.1.call-start
  8.0 22.5 %all-gather.3.cloned.1.call-done = bf16[128,5120]{1,0:T(8,128)(2,1)} async-done(((bf16[128,1280]{1,0:T(8,128)(2,1)}), bf16[128,5120]{1,0:T(8,128)(2,1)}) %all-gather.3.cloned.1.call-update) | async-done | bytes 1310736 | tf_op jit(solution)/shard_map/all_gather | solution.py:460
  30.5 10.3 %convolution_convert_fusion.1.g_ref = bf16[128,1280]{1,0:T(8,128)(2,1)} fusion(bf16[128,5120]{1,0:T(8,128)(2,1)} %all-gather.3.cloned.1.call-done, bf16[1280,5120]{1,0:T(8,128)(2,1)} %param.14), kind=kOutput, calls=%fused_computation.2 | convolution fusion | flops 1677885440 | bytes 14745600 | tf_op jit(solution)/shard_map/dot_general | solution.py:459
  40.7 0.0 all-gather.5.cloned.1.call-update
  40.8 0.0 reduce-scatter.2.cloned.1.call-start
  40.8 0.0 copy-done.2
  40.8 0.6 pad.4.i_ref
  41.4 57.2 %shard_map.111 = (bf16[8,128,1280]{2,1,0:T(8,128)(2,1)}, s32[8,8,128]{2,1,0:T(8,128)}) custom-call(bf16[128,1280]{1,0:T(8,128)(2,1)} %q_ref.1, s32[8,128]{1,0:T(8,128)} %pad.4.i_ref), custom_call_target="tpu_custom_call" | custom-call | tf_op jit(solution)/shard_map/pallas_call | solution.py:122
  98.7 0.8 slice.8
  99.4 0.8 fusion.6
  100.2 0.2 reduce_window_sum.14
  100.4 0.1 convert_reduce_fusion.1
  100.5 0.1 copy.18
  100.6 0.2 select_reduce_fusion.1
  100.8 0.1 copy.17
  100.9 0.1 pad_add_fusion.slots_ref
  101.0 0.0 copy-start.1
  101.0 0.2 slice_reduce_fusion
  101.2 0.1 fusion.5
  101.2 0.7 broadcast_in_dim.61.mask_ref
  101.9 0.0 copy-done.1
  101.9 73.1 %shard_map.112 = (bf16[8,10,128,128]{3,2,1,0:T(8,128)(2,1)}, f32[8,2,16,128]{3,2,1,0:T(8,128)}) custom-call(s32[8,7]{1,0:T(8,128)} %copy-done.1, f32[8,6,128]{2,1,0:T(8,128)} %broadcast_in_dim.61.mask_ref, bf16[1024,1280]{1,0:T(8,128)(2,1)} %bitcast.20, bf16[16,128,1280]{2,1,0:T(8,128)(2,1)} %bitcast.16, bf16[16,128,1280]{2,1,0:T(8,128)(2,1)} %bitcast.18), custom_call_target="tpu_custom_call" | custom-call | flops 4000000000 | bytes 16000000 | tf_op jit(solution)/shard_map/pallas_call | solution.py:219
  175.1 16.8 %shard_map.113 = (bf16[128,1280]{1,0:T(8,128)(2,1)}, f32[128,1280]{1,0:T(8,128)}, f32[8,2,16,128]{3,2,1,0:T(8,128)}) custom-call(bf16[128,1280]{1,0:T(8,128)(2,1)} %q_ref.1, bf16[128,1280]{1,0:T(8,128)(2,1)} %k_ref.1, bf16[128,1280]{1,0:T(8,128)(2,1)} %v_ref.1, bf16[128,1280]{1,0:T(8,128)(2,1)} %convolution_convert_fusion.1.g_ref, ...), custom_call_target="tpu_custom_call" | custom-call | flops 100000000 | bytes 6000000 | tf_op jit(solution)/shard_map/pallas_call | solution.py:304
  191.9 7.8 %convolution_convert_fusion = bf16[128,5120]{1,0:T(8,128)(2,1)} fusion(bf16[128,1280]{1,0:T(8,128)(2,1)} %get-tuple-element.24, bf16[1280,5120]{1,0:T(8,128)(2,1)} %param.14), kind=kOutput, calls=%fused_computation | convolution fusion | flops 1678376960 | bytes 14745600 | tf_op jit(solution)/shard_map/dot_general | solution.py:477
  199.7 0.0 reduce-scatter.2.cloned.1.call-update
  199.7 0.1 select_reduce_fusion
  199.8 0.1 copy.19
  199.9 0.6 broadcast_add_fusion.terms_ref
  200.5 0.0 copy-start
  200.5 0.0 all-gather.5.cloned.1.call-done.g_ref
  200.5 131.5 %shard_map.114 = (bf16[8,128,1280]{2,1,0:T(8,128)(2,1)}, bf16[2048,1280]{1,0:T(8,128)(2,1)}, bf16[2048,1280]{1,0:T(8,128)(2,1)}) custom-call(s32[8,7]{1,0:T(8,128)} %copy-done.1, s32[16,8]{1,0:T(8,128)} %broadcast_add_fusion.terms_ref, f32[8,6,128]{2,1,0:T(8,128)} %broadcast_in_dim.61.mask_ref, bf16[1024,1280]{1,0:T(8,128)(2,1)} %bitcast.21, ...), custom_call_target="tpu_custom_call" | custom-call | flops 10000000000 | bytes 28000000 | tf_op jit(solution)/shard_map/pallas_call | solution.py:409
  332.0 2.2 convert_reduce_fusion
  334.2 0.0 copy-done
  334.2 0.8 add_convert_fusion
  335.0 0.0 reduce-scatter.2.cloned.1.call-done
  335.0 5.2 %copy.26 = bf16[2048,1280]{1,0:T(8,128)(2,1)} copy(bf16[2048,1280]{1,0:T(8,128)(2,1)} %get-tuple-element.42) | data formatting | bytes 10485760
  340.2 5.2 %copy.27 = bf16[2048,1280]{1,0:T(8,128)(2,1)} copy(bf16[2048,1280]{1,0:T(8,128)(2,1)} %get-tuple-element.43) | data formatting | bytes 10485760
  (6 shorter events, 0.0 us)
Async XLA Ops:
  7.2 23.3 %all-gather.3.cloned.1.call-start = ((), (), s32[]{:S(2)}) async-start(), calls=%async_computation.1 | async-start | bytes 1638400 | tf_op jit(solution)/shard_map/all_gather | solution.py:460
  7.9 32.9 %copy-start.2 = (s32[1,32]{1,0:T(1,128)S(1)}, s32[1,32]{1,0:T(1,128)}, u32[]{:S(2)}) copy-start(s32[1,32]{1,0:T(1,128)} %param.13) | copy-start | bytes 388
  7.9 192.6 %all-gather.5.cloned.1.call-start = ((), (), s32[]{:S(2)}) async-start(), calls=%async_computation.3 | async-start | bytes 2949120 | tf_op jit(solution)/shard_map/all_gather | solution.py:465
  40.8 294.2 %reduce-scatter.2.cloned.1.call-start = ((), (), s32[]{:S(2)}) async-start(), calls=%async_computation.2 | async-start | bytes 1638400 | tf_op jit(solution)/shard_map/reduce_scatter | solution.py:479
  101.0 1.0 copy-start.1
  200.5 133.7 %copy-start = (f32[128,1280]{1,0:T(8,128)S(1)}, f32[128,1280]{1,0:T(8,128)}, u32[]{:S(2)}) copy-start(f32[128,1280]{1,0:T(8,128)} %get-tuple-element.29) | copy-start | bytes 1966084
Sparse Core Ops, SparseCore 0:
  9.6 20.8 all-gather.2
  40.9 67.9 all-gather.4
  199.8 25.7 reduce-scatter.1

commit v3 on v2

--- a/solution.py
+++ b/solution.py
@@ -12,6 +12,7 @@
 BLOCK = 128
 R = 32
 STAT_ROWS = 16
+UNROLL = 1
 LOWEST = -1e30
 SCALE = HS ** (-0.5)
 LOG2E = math.log2(math.e)
@@ -129,6 +130,7 @@
         ],
         scratch_shapes=[pltpu.SemaphoreType.DMA((2,))] + [pltpu.SemaphoreType.DMA((2, steps))] * 4,
         compiler_params=remote_params(0),
+        cost_estimate=pl.CostEstimate(flops=2 * 10**10, bytes_accessed=10**8, transcendentals=0),
     )(x, ids)
 
 
@@ -150,23 +152,20 @@
 
     def one_block(b, carry):
         q = q_ref[pl.ds(pl.multiple_of(b * BLOCK, BLOCK), BLOCK), :]
-        scores = []
-        for j in range(capacity):
-            s = dot_last(k_ref[slots_ref[b, j]], q) * (SCALE * LOG2E)
-            scores.append(s + mask_ref[b, j : j + 1, :])
-        peak = jnp.max(functools.reduce(jnp.maximum, scores), axis=0, keepdims=True)
-        weights = [jnp.exp2(s - peak) for s in scores]
-        norm = jnp.sum(functools.reduce(jnp.add, weights), axis=0, keepdims=True)
-        total = None
-        for j in range(capacity):
-            term = dot_plain(vt_ref[slots_ref[b, j]], weights[j].astype(BF16))
-            total = term if total is None else total + term
+        keys = jnp.concatenate([k_ref[slots_ref[b, j]] for j in range(capacity)], axis=0)
+        scores = dot_last(keys, q) * (SCALE * LOG2E)
+        scores = scores.reshape(capacity, BLOCK, BLOCK) + mask_ref[b][:, None, :]
+        peak = jnp.max(jnp.max(scores, axis=0), axis=0, keepdims=True)
+        weights = jnp.exp2(scores - peak)
+        norm = jnp.sum(jnp.sum(weights, axis=0), axis=0, keepdims=True)
+        values = jnp.concatenate([vt_ref[slots_ref[b, j]] for j in range(capacity)], axis=1)
+        total = dot_plain(values, weights.astype(BF16).reshape(capacity * BLOCK, BLOCK))
         part_ref[head, b] = total.astype(BF16)
         stat_ref[b, 0, pl.ds(head, 1), :] = peak
         stat_ref[b, 1, pl.ds(head, 1), :] = norm
         return carry
 
-    lax.fori_loop(0, groups, one_block, 0)
+    lax.fori_loop(0, groups, one_block, 0, unroll=UNROLL)
 
     def part_push(h, peer, owner):
         return push(
@@ -345,20 +344,24 @@
         q, g = q_ref[here, :], g_ref[here, :]
         lse = row_ref[b, 0, pl.ds(head, 1), :]
         delta = row_ref[b, 1, pl.ds(head, 1), :]
-        total = None
-        for j in range(capacity):
-            s = dot_last(k_ref[slots_ref[b, j]], q) * (SCALE * LOG2E)
-            s = s + mask_ref[b, j : j + 1, :]
-            prob = jnp.exp2(s - lse)
-            ds = (prob * (dot_last(v_ref[slots_ref[b, j]], g) - delta)).astype(BF16)
-            term = dot_plain(kt_ref[slots_ref[b, j]], ds)
-            total = term if total is None else total + term
-            dkp_ref[b * capacity + j] = dot_plain(ds, q)
-            dvp_ref[b * capacity + j] = dot_plain(prob.astype(BF16), g)
+        picked = [slots_ref[b, j] for j in range(capacity)]
+        keys = jnp.concatenate([k_ref[slot] for slot in picked], axis=0)
+        values = jnp.concatenate([v_ref[slot] for slot in picked], axis=0)
+        scores = dot_last(keys, q) * (SCALE * LOG2E)
+        scores = scores.reshape(capacity, BLOCK, BLOCK) + mask_ref[b][:, None, :]
+        prob = jnp.exp2(scores - lse)
+        dprob = dot_last(values, g).reshape(capacity, BLOCK, BLOCK)
+        ds = (prob * (dprob - delta)).astype(BF16).reshape(capacity * BLOCK, BLOCK)
+        turned = jnp.concatenate([kt_ref[slot] for slot in picked], axis=1)
+        total = dot_plain(turned, ds)
+        pairs = pl.ds(b * capacity, capacity)
+        shape = (capacity, BLOCK, HS)
+        dkp_ref[pairs] = dot_plain(ds, q).reshape(shape)
+        dvp_ref[pairs] = dot_plain(prob.astype(BF16).reshape(capacity * BLOCK, BLOCK), g).reshape(shape)
         part_ref[head, b] = (total * SCALE).T.astype(BF16)
         return carry
 
-    lax.fori_loop(0, groups, one_block, 0)
+    lax.fori_loop(0, groups, one_block, 0, unroll=UNROLL)
 
     def part_push(h, peer, owner):
         at = pl.ds(pl.multiple_of(h * HS, HS), HS)
@@ -456,8 +459,10 @@
     q_all = q_all.reshape(groups * BLOCK, width)
     slots = owned_slots(ids[:, 0, :R], holder, capacity, stored)
     terms = slot_terms(slots, capacity, stored)
+    whole_grad_out = lax.all_gather(grad_out, "head", axis=1, tiled=True)
+    q_all, whole_grad_out = lax.optimization_barrier((q_all, whole_grad_out))
     grad = lax.dot_general(
-        lax.all_gather(grad_out, "head", axis=1, tiled=True),
+        whole_grad_out,
         out_proj,
         (((1,), (1,)), ((), ())),
         preferred_element_type=F32,

time: 352 us -> 272 us (0.77)
  Pallas kernels: 279 us -> 220 us
  waiting for transfers between devices: 23.3 us -> 0.74 us
    pallas_call x1, Pallas kernels: 131 us -> 66.7 us  [holder_backward(): pl.pallas_call(functools.partial(backward_kernel, groups, heads, capacity...]
    pallas_call x1, Pallas kernels: 73.1 us -> 99.7 us  [holder_forward(): pl.pallas_call(functools.partial(forward_kernel, groups, heads, capacity,...]
    all_gather x1, waiting for transfers between devices: 22.5 us -> 0.02 us  [per_device(): whole_grad_out = lax.all_gather(grad_out, 'head', axis=1, tiled=True)]
    pallas_call x1, Pallas kernels: 57.2 us -> 36.8 us  [ring_gather(): pl.pallas_call(functools.partial(ring_kernel, groups), in_specs=[anywhere...]
    unnamed x8 -> x6, local copies, waits for them, and re-layouts: 10.4 us -> 10.4 us
  transfers between devices with their start and end apart: 3 -> 3, of which waited for: 1 -> 0; matrix products, arithmetic and copies ran while one was open for 4% -> 6% of each run, Pallas kernels for 79% -> 81%
where the time goes in v3:
time: 272 us; the launch traced here: 271 us
  Pallas kernels  220 us (81%)
  matrix products  18 us (7%)
  between operations  13.9 us (5%)
  local copies, waits for them, and re-layouts  13.5 us (5%)
  other arithmetic  5.11 us (2%)
    pallas_call x1, Pallas kernels, holder_forward(): pl.pallas_call(functools.partial(forward_kernel, groups, heads, capacity,...  99.7 us
    pallas_call x1, Pallas kernels, holder_backward(): pl.pallas_call(functools.partial(backward_kernel, groups, heads, capacity...  66.7 us
    pallas_call x1, Pallas kernels, ring_gather(): pl.pallas_call(functools.partial(ring_kernel, groups), in_specs=[anywhere...  36.8 us
    pallas_call x1, Pallas kernels, combine(): pl.pallas_call(functools.partial(combine_kernel, groups, heads), grid=(he...  16.6 us
    unnamed x6, local copies, waits for them, and re-layouts  10.4 us
    dot_general x1, matrix products, per_device(): lax.dot_general(whole_grad_out, out_proj, (((1,), (1,)), ((), ())), prefe...  10.2 us
    dot_general x1, matrix products, per_device(): jnp.dot(attention, out_proj, preferred_element_type=F32).astype(BF16)  7.78 us
  transfers between devices with their start and end apart: 3, of which 0 were waited for; matrix products, arithmetic and copies ran while one was open for 6% of the time, Pallas kernels for 81%

profile of v3, /device:TPU:0, one launch (start us, length us, event | category | flops | bytes accessed | tf_op | source)
XLA Modules:
  0.0 271.2 jit_solution(12545709467537683442)
XLA Ops:
  7.2 0.0 all-gather.3.cloned.1.call-start
  7.2 0.7 all-gather.3.cloned.1.call-update
  7.9 0.0 all-gather.5.cloned.1.call-start
  7.9 1.3 pad.4.i_ref
  9.2 36.8 %shard_map.111 = (bf16[8,128,1280]{2,1,0:T(8,128)(2,1)}, s32[8,8,128]{2,1,0:T(8,128)}) custom-call(bf16[128,1280]{1,0:T(8,128)(2,1)} %q_ref.1, s32[8,128]{1,0:T(8,128)} %pad.4.i_ref), custom_call_target="tpu_custom_call" | custom-call | flops 20000000000 | bytes 100000000 | tf_op jit(solution)/shard_map/pallas_call | solution.py:123
  46.0 0.0 all-gather.3.cloned.1.call-done
  46.0 10.2 %convolution_convert_fusion.1.g_ref = bf16[128,1280]{1,0:T(8,128)(2,1)} fusion(bf16[128,5120]{1,0:T(8,128)(2,1)} %all-gather.3.cloned.1.call-done, bf16[1280,5120]{1,0:T(8,128)(2,1)} %param.14), kind=kOutput, calls=%fused_computation.2 | convolution fusion | flops 1677885440 | bytes 14745600 | tf_op jit(solution)/shard_map/dot_general | solution.py:464
  56.3 0.0 all-gather.5.cloned.1.call-update
  56.3 0.0 reduce-scatter.2.cloned.1.call-start
  56.3 0.8 slice.8
  57.1 0.8 fusion.6
  57.9 0.2 reduce_window_sum.14
  58.1 0.1 convert_reduce_fusion.1
  58.2 0.1 copy.18
  58.3 0.2 select_reduce_fusion.1
  58.5 0.1 copy.17
  58.6 0.1 pad_add_fusion.slots_ref
  58.6 0.0 copy-start.1
  58.6 0.2 slice_reduce_fusion
  58.8 0.1 fusion.5
  58.9 0.7 broadcast_in_dim.61.mask_ref
  59.6 0.0 copy-done.1
  59.6 99.7 %shard_map.112 = (bf16[8,10,128,128]{3,2,1,0:T(8,128)(2,1)}, f32[8,2,16,128]{3,2,1,0:T(8,128)}) custom-call(s32[8,7]{1,0:T(8,128)} %copy-done.1, f32[8,6,128]{2,1,0:T(8,128)} %broadcast_in_dim.61.mask_ref, bf16[1024,1280]{1,0:T(8,128)(2,1)} %bitcast.20, bf16[16,128,1280]{2,1,0:T(8,128)(2,1)} %bitcast.16, bf16[16,128,1280]{2,1,0:T(8,128)(2,1)} %bitcast.18), custom_call_target="tpu_custom_call" | custom-call | flops 4000000000 | bytes 16000000 | tf_op jit(solution)/shard_map/pallas_call | solution.py:218
  159.3 16.6 %shard_map.113 = (bf16[128,1280]{1,0:T(8,128)(2,1)}, f32[128,1280]{1,0:T(8,128)}, f32[8,2,16,128]{3,2,1,0:T(8,128)}) custom-call(bf16[128,1280]{1,0:T(8,128)(2,1)} %q_ref.1, bf16[128,1280]{1,0:T(8,128)(2,1)} %k_ref.1, bf16[128,1280]{1,0:T(8,128)(2,1)} %v_ref.1, bf16[128,1280]{1,0:T(8,128)(2,1)} %convolution_convert_fusion.1.g_ref, ...), custom_call_target="tpu_custom_call" | custom-call | flops 100000000 | bytes 6000000 | tf_op jit(solution)/shard_map/pallas_call | solution.py:303
  176.0 7.8 %convolution_convert_fusion = bf16[128,5120]{1,0:T(8,128)(2,1)} fusion(bf16[128,1280]{1,0:T(8,128)(2,1)} %get-tuple-element.28, bf16[1280,5120]{1,0:T(8,128)(2,1)} %param.14), kind=kOutput, calls=%fused_computation | convolution fusion | flops 1678376960 | bytes 14745600 | tf_op jit(solution)/shard_map/dot_general | solution.py:482
  183.8 0.0 reduce-scatter.2.cloned.1.call-update
  183.8 0.1 select_reduce_fusion
  183.9 0.1 copy.19
  184.0 0.6 broadcast_add_fusion.terms_ref
  184.6 0.0 copy-start
  184.6 0.0 all-gather.5.cloned.1.call-done.g_ref
  184.6 66.7 %shard_map.114 = (bf16[8,128,1280]{2,1,0:T(8,128)(2,1)}, bf16[2048,1280]{1,0:T(8,128)(2,1)}, bf16[2048,1280]{1,0:T(8,128)(2,1)}) custom-call(s32[8,7]{1,0:T(8,128)} %copy-done.1, s32[16,8]{1,0:T(8,128)} %broadcast_add_fusion.terms_ref, f32[8,6,128]{2,1,0:T(8,128)} %broadcast_in_dim.61.mask_ref, bf16[1024,1280]{1,0:T(8,128)(2,1)} %bitcast.21, ...), custom_call_target="tpu_custom_call" | custom-call | flops 10000000000 | bytes 28000000 | tf_op jit(solution)/shard_map/pallas_call | solution.py:412
  251.3 2.2 convert_reduce_fusion
  253.5 0.0 copy-done
  253.5 0.8 add_convert_fusion
  254.3 0.0 reduce-scatter.2.cloned.1.call-done
  254.3 5.2 %copy.26 = bf16[2048,1280]{1,0:T(8,128)(2,1)} copy(bf16[2048,1280]{1,0:T(8,128)(2,1)} %get-tuple-element.46) | data formatting | bytes 10485760
  259.5 5.2 %copy.27 = bf16[2048,1280]{1,0:T(8,128)(2,1)} copy(bf16[2048,1280]{1,0:T(8,128)(2,1)} %get-tuple-element.47) | data formatting | bytes 10485760
  (6 shorter events, 0.0 us)
Async XLA Ops:
  7.2 38.8 %all-gather.3.cloned.1.call-start = ((), (), s32[]{:S(2)}) async-start(), calls=%async_computation.1 | async-start | bytes 1638400 | tf_op jit(solution)/shard_map/all_gather | solution.py:462
  7.9 176.7 %all-gather.5.cloned.1.call-start = ((), (), s32[]{:S(2)}) async-start(), calls=%async_computation.3 | async-start | bytes 2949120 | tf_op jit(solution)/shard_map/all_gather | solution.py:470
  56.3 198.0 %reduce-scatter.2.cloned.1.call-start = ((), (), s32[]{:S(2)}) async-start(), calls=%async_computation.2 | async-start | bytes 1638400 | tf_op jit(solution)/shard_map/reduce_scatter | solution.py:484
  58.6 1.0 copy-start.1
  184.6 68.9 %copy-start = (f32[128,1280]{1,0:T(8,128)S(1)}, f32[128,1280]{1,0:T(8,128)}, u32[]{:S(2)}) copy-start(f32[128,1280]{1,0:T(8,128)} %get-tuple-element.33) | copy-start | bytes 1966084
Sparse Core Ops, SparseCore 0:
  9.6 20.8 all-gather.2
  56.4 89.5 all-gather.4
  183.9 25.9 reduce-scatter.1
